TPU v7x, 32 devices: a whole 2x2x4 slice. The times are simulated.
32 devices in a mesh: scen: 8 (over y, x, core), fs: 4 (over z).
Axes of the slice: x: 2, y: 2, z: 4, core: 2. Of those that a mesh axis runs over, the one named last changes fastest.
Arguments:
- scen_rhs: float32 [64, 64, 64, 128], P('scen', 'fs')
- first_rhs: float32 [4, 4096, 128], P('fs', 'scen'), may hold values from -6 to 6
- diag_blocks: float32 [64, 64, 64, 64], P('scen', 'fs')
- diag_inverse: bfloat16 [64, 64, 64, 64], P('scen', 'fs')
- couplings: float32 [64, 64, 2, 64, 64], P('scen', 'fs'), may hold values from -0.125 to 0.125
- border: float32 [64, 64, 64, 64], P('scen', 'fs'), may hold values from -0.125 to 0.125
- border_block: int32 [64, 64], P('scen', 'fs'), may hold values from 0 to 63
- first_diag: float32 [4, 4096], P('fs', 'scen'), may hold values from 0.5 to 2
- schur_inverse: bfloat16 [4, 4096, 4, 4096], P(None, 'scen', 'fs')
Outputs:
- scen_sol: float32 [64, 64, 64, 128], P('scen', 'fs')
- first_sol: float32 [4, 4096, 128], P('fs', 'scen')
- first_res: float32 [4, 4096, 128], P('fs', 'scen')
All inputs are finite; a program needn't handle non-finite values.
Results may differ from a plain program's by a relative error of at most 0.0049.
Values may be sent and summed in bfloat16 or wider, within the bound.
A program may use at most 128 MiB of HBM per device.

v0:
```python
import jax
import jax.numpy as jnp
from jax import lax
from jax.sharding import PartitionSpec as P

ROUNDS = 2


EXACT = lax.Precision.HIGHEST


def with_halo(cells, sides, width):
    for axis, dim in sides:
        count = lax.axis_size(axis)
        ends = count - 1
        head = lax.slice_in_dim(cells, 0, width, axis=dim)
        tail = lax.slice_in_dim(cells, cells.shape[dim] - width, cells.shape[dim], axis=dim)
        cells = jnp.concatenate(
            [
                lax.ppermute(tail, axis, [(i, (i + 1) % count) for i in range(ends)]),
                cells,
                lax.ppermute(head, axis, [((i + 1) % count, i) for i in range(ends)]),
            ],
            axis=dim,
        )
    return cells


def tile_product(mats, values):
    return jnp.einsum("swij,swjr->swir", mats, values, precision=EXACT)


def tile_transpose(mats, values):
    return jnp.einsum("swji,swjr->swir", mats, values, precision=EXACT)


def low_product(mats, values):
    return jnp.einsum("swij,swjr->swir", mats, values, preferred_element_type=jnp.float32)


def per_device(
    scen_rhs,
    first_rhs,
    diag_blocks,
    diag_inverse,
    couplings,
    border,
    border_block,
    first_diag,
    schur_inverse,
):
    position = lax.axis_index("scen")
    window_size = diag_blocks.shape[-1]
    group_rows = schur_inverse.shape[-1]
    own_rows = first_rhs.shape[1]
    rhs_count = scen_rhs.shape[-1]
    block_count = group_rows // window_size
    scen_local = border_block.shape[0]
    window_local = border_block.shape[1]
    slot_count = scen_local * window_local
    selector = (
        border_block.reshape(1, slot_count) == jnp.arange(block_count, dtype=jnp.int32)[:, None]
    ).astype(jnp.float32)
    columns = schur_inverse.shape[0] * schur_inverse.shape[1]
    schur_flat = schur_inverse.reshape(columns, group_rows)
    first_gain = first_diag.reshape(own_rows, 1)
    row_start = position * own_rows

    def collect(values):
        terms = tile_transpose(border, values).reshape(slot_count, window_size * rhs_count)
        partial_value = jnp.dot(selector, terms, precision=EXACT).reshape(group_rows, rhs_count)
        return lax.psum_scatter(partial_value, "scen", scatter_dimension=0, tiled=True)

    scen_res = scen_rhs
    first_res = first_rhs.reshape(own_rows, rhs_count)
    scen_sol = jnp.zeros(scen_rhs.shape, jnp.float32)
    first_sol = jnp.zeros((own_rows, rhs_count), jnp.float32)
    for round_index in range(ROUNDS):
        guess = low_product(diag_inverse, scen_res.astype(jnp.bfloat16))
        schur_rhs = (first_res + collect(guess)).astype(jnp.bfloat16)
        operand = schur_rhs.reshape(1, own_rows, rhs_count)
        gathered = lax.all_gather(operand, "fs", axis=0, tiled=True).reshape(columns, rhs_count)
        solve_partial_value = lax.dot_general(
            schur_flat, gathered, (((0,), (0,)), ((), ())), preferred_element_type=jnp.float32
        )
        summed = lax.psum(solve_partial_value, "scen")
        owned = lax.dynamic_slice_in_dim(summed, row_start, own_rows, 0)
        group_blocks = summed.reshape(block_count, window_size * rhs_count)
        widened = lax.dot_general(selector, group_blocks, (((0,), (0,)), ((), ())), precision=EXACT)
        widened = widened.reshape(scen_local, window_local, window_size, rhs_count)
        coupled = tile_product(border, widened)
        scen_step = guess - low_product(diag_inverse, coupled.astype(jnp.bfloat16))
        padded = with_halo(scen_step, (("fs", 1),), 1)
        before = padded[:, :-2]
        after = padded[:, 2:]
        image_scen = tile_product(diag_blocks, scen_step) + tile_product(couplings[:, :, 0], before)
        image_scen = image_scen + tile_product(couplings[:, :, 1], after) + coupled
        image_first = first_gain * owned - collect(scen_step)
        along = jnp.sum(scen_res * image_scen, axis=(0, 1, 2)) + jnp.sum(
            first_res * image_first, axis=0
        )
        energy = jnp.sum(image_scen * image_scen, axis=(0, 1, 2)) + jnp.sum(
            image_first * image_first, axis=0
        )
        along, energy = lax.psum((along, energy), ("scen", "fs"))
        step_size = along / (energy + 1e-06)
        scen_sol = scen_sol + step_size * scen_step
        first_sol = first_sol + step_size * owned
        scen_res = scen_res - step_size * image_scen
        first_res = first_res - step_size * image_first
    return (
        scen_sol,
        first_sol.reshape(1, own_rows, rhs_count),
        first_res.reshape(1, own_rows, rhs_count),
    )


def solution(mesh):
    return jax.shard_map(
        per_device,
        mesh=mesh,
        in_specs=(
            P("scen", "fs", None, None),
            P("fs", "scen", None),
            P("scen", "fs", None, None),
            P("scen", "fs", None, None),
            P("scen", "fs", None, None, None),
            P("scen", "fs", None, None),
            P("scen", "fs"),
            P("fs", "scen"),
            P(None, "scen", "fs", None),
        ),
        out_specs=(P("scen", "fs", None, None), P("fs", "scen", None), P("fs", "scen", None)),
        check_vma=False,
    )
```

profile of v0, /device:TPU:0, one launch (start us, length us, event | category | flops | bytes accessed | tf_op | source)
XLA Modules:
  0.0 574.7 jit_solution(9570922974804120888)
XLA Ops:
  8.8 3.0 fusion.53
  12.2 7.2 %fusion.81 = f32[8,16,128,64]{2,3,1,0:T(8,128)S(1)} fusion(f32[8,16,64,128]{3,2,1,0:T(8,128)S(1)} %fusion.53, f32[8,16,64,64]{3,2,1,0:T(8,128)S(1)} %copy-done.1), kind=kOutput, calls=%fused_computation.97 | convolution fusion | flops 805306368 | bytes 10485760 | tf_op jit(solution)/shard_map/swji,swjr->swir/dot_general | solution.py:34
  19.5 5.4 fusion.25
  24.9 3.0 reshape.95
  27.9 3.0 copy.24
  31.1 43.9 %reduce-scatter.5.cloned.1.call-done = f32[512,128]{0,1:T(8,128)} async-done(((f32[4096,128]{0,1:T(8,128)}), f32[512,128]{0,1:T(8,128)}) %reduce-scatter.5.cloned.1.call-update) | async-done | bytes 262160 | tf_op jit(solution)/shard_map/reduce_scatter | solution.py:72
  76.0 15.7 %all-gather = bf16[2048,128]{0,1:T(8,128)(2,1)S(1)} all-gather(bf16[512,128]{0,1:T(8,128)(2,1)S(1)} %fusion.64), channel_id=2, replica_groups=mesh['scen'=8,'fs'=4] {'fs'}, dimensions={0}, use_global_device_ids=true | all-gather | bytes 655360 | tf_op jit(solution)/shard_map/all_gather | solution.py:82
  91.6 9.5 %convolution_bitcast_fusion.1 = f32[4096,128]{0,1:T(8,128)} fusion(bf16[2048,128]{0,1:T(8,128)(2,1)S(1)} %all-gather, bf16[2048,4096]{1,0:T(8,128)(2,1)} %bitcast.132), kind=kOutput, calls=%fused_computation.1 | convolution fusion | flops 2147483648 | bytes 19398656 | tf_op jit(solution)/shard_map/dot_general | solution.py:83
  101.2 62.3 %all-reduce.5.cloned.1.call-done = f32[4096,128]{0,1:T(8,128)} async-done(((f32[4096,128]{0,1:T(8,128)}), f32[4096,128]{0,1:T(8,128)}) %all-reduce.5.cloned.1.call-update) | async-done | bytes 2097168 | tf_op jit(solution)/shard_map/psum | solution.py:86
  163.5 2.9 copy.25
  166.4 2.7 reshape.99
  169.1 2.0 copy.49
  171.1 3.2 fusion.47
  174.4 6.3 %fusion.39 = f32[8,16,128,64]{2,3,1,0:T(8,128)S(1)} fusion(f32[8,16,64,64]{3,2,1,0:T(8,128)S(1)} %copy-done.2, f32[8,16,64,128]{3,1,2,0:T(8,128)S(1)} %fusion.47), kind=kOutput, calls=%fused_computation.47 | convolution fusion | flops 805306368 | bytes 10485760 | tf_op jit(solution)/shard_map/swij,swjr->swir/dot_general | solution.py:30
  182.7 7.4 %fusion.83 = f32[8,16,128,64]{2,3,1,0:T(8,128)S(1)} fusion(f32[8,16,64,128]{3,2,1,0:T(8,128)S(1)} %bitcast_subtract_fusion, f32[8,16,64,64]{3,2,1,0:T(8,128)S(1)} %copy-done.2), kind=kOutput, calls=%fused_computation.99 | convolution fusion | flops 805306368 | bytes 10485760 | tf_op jit(solution)/shard_map/swji,swjr->swir/dot_general | solution.py:34
  190.1 5.4 fusion.22
  195.5 2.7 reshape.101
  198.2 2.9 copy.29
  203.6 5.2 collective-permute-start
  208.8 10.0 %fusion.82 = f32[8,16,128,64]{2,3,1,0:T(8,128)} fusion(f32[8,16,64,128]{3,2,1,0:T(8,128)} %copy-done.5, f32[8,16,64,64]{3,2,1,0:T(8,128)} %param.11), kind=kOutput, calls=%fused_computation.98 | convolution fusion | flops 805306368 | bytes 10485760 | tf_op jit(solution)/shard_map/swij,swjr->swir/dot_general | solution.py:30
  218.9 8.6 %fusion = f32[8,16,128,64]{2,3,1,0:T(8,128)} fusion(f32[8,16,64,128]{3,2,1,0:T(8,128)S(1)} %copy-done.6, f32[8,1,64,128]{3,2,1,0:T(8,128)S(1)} %collective-permute-done, f32[8,16,2,64,64]{4,3,2,1,0:T(8,128)} %param.13), kind=kOutput, calls=%fused_computation.2 | convolution fusion | flops 806420480 | bytes 12845056 | tf_op jit(solution)/shard_map/swij,swjr->swir/dot_general | solution.py:30
  227.4 13.1 %fusion.35 = (f32[128]{0:T(128)S(1)}, f32[128]{0:T(128)S(1)}, f32[8,16,128,64]{2,3,1,0:T(8,128)}) fusion(f32[8,16,64,128]{3,2,1,0:T(8,128)} %param.9, f32[8,16,128,64]{2,3,1,0:T(8,128)S(1)} %copy-done.14, f32[8,16,2,64,64]{4,3,2,1,0:T(8,128)} %param.13, f32[8,1,64,128]{3,2,1,0:T(8,128)S(1)} %collective-permute-done.1, f32[8,16,64,128]{3,2,1,0:T(8,128)S(1)} %copy-done.6, ...), kind=kOutput, calls=%fused_computation.42 | convolution fusion | flops 813760256 | bytes 29623296 | tf_op jit(solution)/shard_map/swij,swjr->swir/dot_general | solution.py:30
  242.9 39.4 %all-reduce.1 = (f32[128]{0:T(128)S(1)}, f32[128]{0:T(128)S(1)}) all-reduce(f32[128]{0:T(128)S(1)} %add.88, f32[128]{0:T(128)S(1)} %add.89), channel_id=1, replica_groups=mesh['scen'=8,'fs'=4] {'scen','fs'}, use_global_device_ids=true, to_apply=%region_5.0 | all-reduce | flops 256 | bytes 2048 | tf_op jit(solution)/shard_map/psum | solution.py:105
  282.3 4.3 fusion.50
  287.0 7.2 %fusion.84 = f32[8,16,128,64]{2,3,1,0:T(8,128)S(1)} fusion(f32[8,16,128,64]{2,3,1,0:T(8,128)S(1)} %fusion.50, f32[8,16,64,64]{3,2,1,0:T(8,128)S(1)} %copy-done.3), kind=kOutput, calls=%fused_computation.100 | convolution fusion | flops 805306368 | bytes 10485760 | tf_op jit(solution)/shard_map/swji,swjr->swir/dot_general | solution.py:34
  294.2 5.4 fusion.19
  299.6 3.1 reshape.103
  302.7 2.9 copy.31
  305.7 42.0 %reduce-scatter.9.cloned.1.call-done = f32[512,128]{0,1:T(8,128)} async-done(((f32[4096,128]{0,1:T(8,128)}), f32[512,128]{0,1:T(8,128)}) %reduce-scatter.9.cloned.1.call-update) | async-done | bytes 262160 | tf_op jit(solution)/shard_map/reduce_scatter | solution.py:72
  348.8 15.6 %all-gather.1 = bf16[2048,128]{0,1:T(8,128)(2,1)S(1)} all-gather(bf16[512,128]{0,1:T(8,128)(2,1)S(1)} %get-tuple-element.22), channel_id=3, replica_groups=mesh['scen'=8,'fs'=4] {'fs'}, dimensions={0}, use_global_device_ids=true | all-gather | bytes 655360 | tf_op jit(solution)/shard_map/all_gather | solution.py:82
  364.4 9.5 %convolution_bitcast_fusion = f32[4096,128]{0,1:T(8,128)} fusion(bf16[2048,128]{0,1:T(8,128)(2,1)S(1)} %all-gather.1, bf16[2048,4096]{1,0:T(8,128)(2,1)} %bitcast.133), kind=kOutput, calls=%fused_computation | convolution fusion | flops 2147483648 | bytes 19398656 | tf_op jit(solution)/shard_map/dot_general | solution.py:83
  374.0 62.3 %all-reduce.7.cloned.1.call-done = f32[4096,128]{0,1:T(8,128)} async-done(((f32[4096,128]{0,1:T(8,128)}), f32[4096,128]{0,1:T(8,128)}) %all-reduce.7.cloned.1.call-update) | async-done | bytes 2097168 | tf_op jit(solution)/shard_map/psum | solution.py:86
  436.3 2.9 copy.32
  439.2 2.8 reshape.106
  442.0 2.0 copy.52
  443.9 3.2 fusion.45
  447.2 6.3 %fusion.37 = f32[8,16,128,64]{2,3,1,0:T(8,128)S(1)} fusion(f32[8,16,64,64]{3,2,1,0:T(8,128)S(1)} %copy-done.4, f32[8,16,64,128]{3,1,2,0:T(8,128)S(1)} %fusion.45), kind=kOutput, calls=%fused_computation.45 | convolution fusion | flops 805306368 | bytes 10485760 | tf_op jit(solution)/shard_map/swij,swjr->swir/dot_general | solution.py:30
  455.5 7.4 %fusion.86 = f32[8,16,128,64]{2,3,1,0:T(8,128)S(1)} fusion(f32[8,16,128,64]{2,3,1,0:T(8,128)S(1)} %convolution_subtract_fusion, f32[8,16,64,64]{3,2,1,0:T(8,128)S(1)} %copy-done.4), kind=kOutput, calls=%fused_computation.102 | convolution fusion | flops 805306368 | bytes 10485760 | tf_op jit(solution)/shard_map/swji,swjr->swir/dot_general | solution.py:34
  463.0 3.4 collective-permute-start.2
  466.4 5.4 fusion.16
  471.8 2.7 reshape.108
  474.5 2.9 copy.34
  477.5 9.8 %fusion.85 = f32[8,16,128,64]{2,3,1,0:T(8,128)} fusion(f32[8,16,128,64]{2,3,1,0:T(8,128)} %copy-done.7, f32[8,16,64,64]{3,2,1,0:T(8,128)} %param.11), kind=kOutput, calls=%fused_computation.101 | convolution fusion | flops 805306368 | bytes 10485760 | tf_op jit(solution)/shard_map/swij,swjr->swir/dot_general | solution.py:30
  488.8 8.4 %fusion.8 = f32[8,16,128,64]{2,3,1,0:T(8,128)} fusion(f32[8,16,64,128]{3,2,1,0:T(8,128)S(1)} %bitcast.135, f32[8,1,64,128]{3,2,1,0:T(8,128)S(1)} %collective-permute-done.2, f32[8,16,2,64,64]{4,3,2,1,0:T(8,128)} %param.13), kind=kOutput, calls=%fused_computation.10 | convolution fusion | flops 806420480 | bytes 12845056 | tf_op jit(solution)/shard_map/swij,swjr->swir/dot_general | solution.py:30
  497.2 13.9 %fusion.33 = (f32[128]{0:T(128)S(1)}, f32[128]{0:T(128)S(1)}) fusion(f32[8,16,64,128]{3,2,1,0:T(8,128)} %param.9, f32[8,16,128,64]{2,3,1,0:T(8,128)} %get-tuple-element.31, f32[128]{0:T(128)S(1)} %add_divide_fusion.1, f32[8,16,128,64]{2,3,1,0:T(8,128)} %copy-done.15, f32[8,16,2,64,64]{4,3,2,1,0:T(8,128)} %param.13, ...), kind=kOutput, calls=%fused_computation.37 | convolution fusion | flops 815857408 | bytes 29623808 | tf_op jit(solution)/shard_map/swij,swjr->swir/dot_general | solution.py:30
  511.1 6.0 %reduce-scatter.11.cloned.1.call-done = f32[512,128]{0,1:T(8,128)} async-done(((f32[4096,128]{0,1:T(8,128)}), f32[512,128]{0,1:T(8,128)}) %reduce-scatter.11.cloned.1.call-update) | async-done | bytes 262160 | tf_op jit(solution)/shard_map/reduce_scatter | solution.py:72
  518.3 39.4 %all-reduce = (f32[128]{0:T(128)S(1)}, f32[128]{0:T(128)S(1)}) all-reduce(f32[128]{0:T(128)S(1)} %add.96, f32[128]{0:T(128)S(1)} %add.97), channel_id=1, replica_groups=mesh['scen'=8,'fs'=4] {'scen','fs'}, use_global_device_ids=true, to_apply=%region_14.0 | all-reduce | flops 256 | bytes 2048 | tf_op jit(solution)/shard_map/psum | solution.py:105
  557.7 7.0 %multiply_add_fusion = f32[8,16,64,128]{3,2,1,0:T(8,128)} fusion(f32[8,16,64,128]{3,2,1,0:T(8,128)} %copy-done.5, f32[128]{0:T(128)S(1)} %add_divide_fusion, f32[128]{0:T(128)S(1)} %add_divide_fusion.1, f32[8,16,128,64]{2,3,1,0:T(8,128)} %copy-done.7), kind=kLoop, calls=%fused_computation.49 | loop fusion | flops 3145728 | bytes 12583936 | tf_op jit(solution)/shard_map/add | solution.py:107
  (76 shorter events, 19.0 us)
Async XLA Ops:
  7.2 1.6 copy-start
  7.2 67.8 %reduce-scatter.5.cloned.1.call-start = ((), (), s32[]{:S(2)}) async-start(), calls=%async_computation.4 | async-start | bytes 2359296 | tf_op jit(solution)/shard_map/reduce_scatter | solution.py:72
  8.8 3.4 copy-start.1
  12.2 7.2 %copy-start.11 = (f32[8,16,64,128]{3,2,1,0:T(8,128)}, f32[8,16,64,128]{3,2,1,0:T(8,128)S(1)}, u32[]{:S(2)}) copy-start(f32[8,16,64,128]{3,2,1,0:T(8,128)S(1)} %fusion.53) | copy-start | bytes 12582916
  27.9 3.1 copy-start.16
  30.9 132.6 %all-reduce.5.cloned.1.call-start = ((), (), s32[]{:S(2)}) async-start(), calls=%async_computation.5 | async-start | bytes 4194304 | tf_op jit(solution)/shard_map/psum | solution.py:86
  101.1 140.6 %reduce-scatter.7.cloned.1.call-start = ((), (), s32[]{:S(2)}) async-start(), calls=%async_computation.6 | async-start | bytes 2359296 | tf_op jit(solution)/shard_map/reduce_scatter | solution.py:72
  166.4 4.7 copy-start.17
  171.1 3.2 copy-start.2
  174.3 6.4 %copy-start.12 = (f32[8,16,64,128]{3,2,1,0:T(8,128)S(1)}, f32[8,16,64,128]{3,2,1,0:T(8,128)}, u32[]{:S(2)}) copy-start(f32[8,16,64,128]{3,2,1,0:T(8,128)} %copy-done.11) | copy-start | bytes 12582916
  180.7 1.9 copy-start.13
  182.7 7.4 %copy-start.5 = (f32[8,16,64,128]{3,2,1,0:T(8,128)}, f32[8,16,64,128]{3,2,1,0:T(8,128)S(1)}, u32[]{:S(2)}) copy-start(f32[8,16,64,128]{3,2,1,0:T(8,128)S(1)} %bitcast_subtract_fusion) | copy-start | bytes 12582916
  201.2 146.6 %reduce-scatter.9.cloned.1.call-start = ((), (), s32[]{:S(2)}) async-start(), calls=%async_computation.7 | async-start | bytes 2359296 | tf_op jit(solution)/shard_map/reduce_scatter | solution.py:72
  202.3 25.2 %collective-permute-start.1 = (f32[8,1,64,128]{3,2,1,0:T(8,128)S(1)}, f32[8,1,64,128]{3,2,1,0:T(8,128)S(1)}, u32[]{:S(2)}, u32[]{:S(2)}) collective-permute-start(f32[8,1,64,128]{3,2,1,0:T(8,128)S(1)} %get-tuple-element.27), channel_id=1, source_target_pairs={{1,0},{2,1},{3,2},{5,4},{6,5},{7,6},{9,8},{10,9},{11,10},{13,12},{... | collective-permute-start | bytes 786440 | tf_op jit(solution)/shard_map/ppermute | solution.py:22
  203.6 15.3 %copy-start.6 = (f32[8,16,64,128]{3,2,1,0:T(8,128)S(1)}, f32[8,16,64,128]{3,2,1,0:T(8,128)}, u32[]{:S(2)}) copy-start(f32[8,16,64,128]{3,2,1,0:T(8,128)} %copy-done.5) | copy-start | bytes 12582916
  203.6 15.3 %collective-permute-start = (f32[8,1,64,128]{3,2,1,0:T(8,128)S(1)}, f32[8,1,64,128]{3,2,1,0:T(8,128)S(1)}, u32[]{:S(2)}, u32[]{:S(2)}) collective-permute-start(f32[8,1,64,128]{3,2,1,0:T(8,128)S(1)} %get-tuple-element.28), channel_id=1, source_target_pairs={{0,1},{1,2},{2,3},{4,5},{5,6},{6,7},{8,9},{9,10},{10,11},{12,13},{... | collective-permute-start | bytes 786440 | tf_op jit(solution)/shard_map/ppermute | solution.py:20
  218.9 8.6 %copy-start.14 = (f32[8,16,128,64]{2,3,1,0:T(8,128)S(1)}, f32[8,16,128,64]{2,3,1,0:T(8,128)}, u32[]{:S(2)}) copy-start(f32[8,16,128,64]{2,3,1,0:T(8,128)} %copy-done.13) | copy-start | bytes 12582916
  227.4 14.3 %copy-start.18 = (f32[1,512]{1,0:T(1,128)S(1)}, f32[1,512]{1,0:T(1,128)}, u32[]{:S(2)}) copy-start(f32[1,512]{1,0:T(1,128)} %param.16) | copy-start | bytes 6148
  282.3 4.6 copy-start.3
  287.0 7.2 %copy-start.9 = (f32[8,16,128,64]{2,3,1,0:T(8,128)}, f32[8,16,128,64]{2,3,1,0:T(8,128)S(1)}, u32[]{:S(2)}) copy-start(f32[8,16,128,64]{2,3,1,0:T(8,128)S(1)} %fusion.50) | copy-start | bytes 12582916
  305.6 130.7 %all-reduce.7.cloned.1.call-start = ((), (), s32[]{:S(2)}) async-start(), calls=%async_computation.8 | async-start | bytes 4194304 | tf_op jit(solution)/shard_map/psum | solution.py:86
  373.9 143.2 %reduce-scatter.11.cloned.1.call-start = ((), (), s32[]{:S(2)}) async-start(), calls=%async_computation.9 | async-start | bytes 2359296 | tf_op jit(solution)/shard_map/reduce_scatter | solution.py:72
  443.9 3.2 copy-start.4
  447.2 6.4 %copy-start.10 = (f32[8,16,128,64]{2,3,1,0:T(8,128)S(1)}, f32[8,16,128,64]{2,3,1,0:T(8,128)}, u32[]{:S(2)}) copy-start(f32[8,16,128,64]{2,3,1,0:T(8,128)} %copy-done.9) | copy-start | bytes 12582916
  453.5 2.0 copy-start.15
  455.5 7.4 %copy-start.7 = (f32[8,16,128,64]{2,3,1,0:T(8,128)}, f32[8,16,128,64]{2,3,1,0:T(8,128)S(1)}, u32[]{:S(2)}) copy-start(f32[8,16,128,64]{2,3,1,0:T(8,128)S(1)} %convolution_subtract_fusion) | copy-start | bytes 12582916
  463.0 25.8 %collective-permute-start.2 = (f32[8,1,64,128]{3,2,1,0:T(8,128)S(1)}, f32[8,1,64,128]{3,2,1,0:T(8,128)S(1)}, u32[]{:S(2)}, u32[]{:S(2)}) collective-permute-start(f32[8,1,64,128]{3,2,1,0:T(8,128)S(1)} %get-tuple-element.26), channel_id=1, source_target_pairs={{0,1},{1,2},{2,3},{4,5},{5,6},{6,7},{8,9},{9,10},{10,11},{12,13},{... | collective-permute-start | bytes 786440 | tf_op jit(solution)/shard_map/ppermute | solution.py:20
  477.5 11.3 %copy-start.8 = (f32[8,16,128,64]{2,3,1,0:T(8,128)S(1)}, f32[8,16,128,64]{2,3,1,0:T(8,128)}, u32[]{:S(2)}) copy-start(f32[8,16,128,64]{2,3,1,0:T(8,128)} %copy-done.7) | copy-start | bytes 12582916
  487.2 10.0 %collective-permute-start.3 = (f32[8,1,64,128]{3,2,1,0:T(8,128)S(1)}, f32[8,1,64,128]{3,2,1,0:T(8,128)S(1)}, u32[]{:S(2)}, u32[]{:S(2)}) collective-permute-start(f32[8,1,64,128]{3,2,1,0:T(8,128)S(1)} %get-tuple-element.25), channel_id=1, source_target_pairs={{1,0},{2,1},{3,2},{5,4},{6,5},{7,6},{9,8},{10,9},{11,10},{13,12},{... | collective-permute-start | bytes 786440 | tf_op jit(solution)/shard_map/ppermute | solution.py:22
Sparse Core Ops, SparseCore 0:
  31.0 43.8 reduce-scatter.4
  101.2 62.1 all-reduce.4
  201.3 40.4 reduce-scatter.6
  305.8 41.9 reduce-scatter.8
  374.0 62.2 all-reduce.6
  477.6 39.4 reduce-scatter.10
where the time goes:
time: 584 us; the launch traced here: 575 us
  waiting for transfers between devices  218 us (37%)
  matrix products  162 us (28%)
  blocking collectives  110 us (19%)
  local copies, waits for them, and re-layouts  46.1 us (8%)
  between operations  14.9 us (3%)
  other arithmetic  12.5 us (2%)
  starting transfers between devices  11.7 us (2%)
    psum x2, waiting for transfers between devices, per_device(): summed = lax.psum(solve_partial_value, 'scen')  125 us
    reduce_scatter x4, waiting for transfers between devices, collect(): lax.psum_scatter(partial_value, 'scen', scatter_dimension=0, tiled=True)  93.1 us
    psum x2, blocking collectives, per_device(): along, energy = lax.psum((along, energy), ('scen', 'fs'))  78.8 us
    dot_general x8, matrix products, tile_product(): return jnp.einsum('swij,swjr->swir', mats, values, precision=EXACT)  76.5 us
    all_gather x2, blocking collectives, per_device(): lax.all_gather(operand, 'fs', axis=0, tiled=True)  31.3 us
    dot_general x4, matrix products, tile_transpose(): return jnp.einsum('swji,swjr->swir', mats, values, precision=EXACT)  29.2 us
    reshape x8, local copies, waits for them, and re-layouts, collect(): jnp.dot(selector, terms, precision=EXACT).reshape(group_rows, rhs_count)  23.3 us
    dot_general x4, matrix products, collect(): jnp.dot(selector, terms, precision=EXACT).reshape(group_rows, rhs_count)  21.7 us
  transfers between devices with their start and end apart: 10, of which 6 were waited for; matrix products, arithmetic and copies ran while one was open for 13% of the time, Pallas kernels for 0%

commit v1 on v0

v1 whole, which is shorter than its diff:
```python
import functools

import jax
import jax.numpy as jnp
from jax import lax
from jax.experimental import pallas as pl
from jax.experimental.pallas import tpu as pltpu
from jax.sharding import PartitionSpec as P

ROUNDS = 2
MIB = 1024 * 1024
MESH = pl.DeviceIdType.MESH
F32 = jnp.float32
BF16 = jnp.bfloat16
VMEM = pl.BlockSpec(memory_space=pltpu.VMEM)
ANY = pl.BlockSpec(memory_space=pl.ANY)


def dot(a, b):
    return jnp.dot(a, b, preferred_element_type=F32)


def dot_t(a, b):
    return lax.dot_general(a, b, (((0,), (0,)), ((), ())), preferred_element_type=F32)


def split(x):
    hi = x.astype(BF16)
    return hi, (x - hi.astype(F32)).astype(BF16)


def guess_kernel(update, size, *refs):
    if update:
        blk, res, image, scale, inv, border, res_out, guess, part, acc = refs
    else:
        blk, res, inv, border, guess, part, acc = refs
    s = pl.program_id(0)
    count = res.shape[1]

    @pl.when(s == 0)
    def _():
        acc[...] = jnp.zeros_like(acc)

    guesses = []
    for w in range(count):
        value = res[0, w]
        if update:
            value = value - scale[...] * image[0, w]
            res_out[0, w] = value
        guesses.append(dot(inv[0, w], value.astype(BF16)))
    terms = []
    for w in range(count):
        guess[0, w] = guesses[w]
        terms.append(dot_t(border[0, w].astype(BF16), guesses[w].astype(BF16)))
    for w in range(count):
        rows = pl.ds(pl.multiple_of(blk[s, w] * size, size), size)
        acc[rows, :] += terms[w]

    @pl.when(s == pl.num_programs(0) - 1)
    def _():
        part[...] = acc[...].astype(BF16)


def step_kernel(size, blk, guess, inv, border, group, step, coupled, part):
    s = pl.program_id(0)
    count = guess.shape[1]

    @pl.when(s == 0)
    def _():
        part[...] = jnp.zeros_like(part)

    places, lifted, borders, terms = [], [], [], []
    for w in range(count):
        rows = pl.ds(pl.multiple_of(blk[s, w] * size, size), size)
        places.append(rows)
        first = group[rows, :]
        hi, lo = split(border[0, w])
        borders.append((hi, lo))
        value = dot(hi, first) + dot(lo, first)
        coupled[0, w] = value
        lifted.append(value.astype(BF16))
    for w in range(count):
        value = guess[0, w] - dot(inv[0, w], lifted[w])
        step[0, w] = value
        vh, vl = split(value)
        hi, lo = borders[w]
        left = jnp.concatenate([hi, lo, hi], axis=0)
        right = jnp.concatenate([vh, vh, vl], axis=0)
        terms.append(dot_t(left, right))
    for w in range(count):
        part[places[w], :] += terms[w]


def by_scenario(shape):
    zeros = (0,) * (len(shape) - 1)
    return pl.BlockSpec((1,) + tuple(shape[1:]), lambda s: (s,) + zeros)


def fixed(shape):
    zeros = (0,) * len(shape)
    return pl.BlockSpec(tuple(shape), lambda s: zeros)


SMEM = pl.BlockSpec(memory_space=pltpu.SMEM)


def guess_call(blk, res, inv, border, rows, image=None, scale=None):
    size, width = res.shape[2:]
    update = image is not None
    field = by_scenario(res.shape)
    ops = [blk, res] + ([image, scale] if update else []) + [inv, border]
    specs = [SMEM, field] + ([field, fixed(scale.shape)] if update else [])
    specs += [by_scenario(inv.shape), by_scenario(border.shape)]
    full = jax.ShapeDtypeStruct(res.shape, F32)
    outs = ([full] if update else []) + [full, jax.ShapeDtypeStruct((rows, width), BF16)]
    out_specs = ([field] if update else []) + [field, fixed((rows, width))]
    return pl.pallas_call(
        functools.partial(guess_kernel, update, size),
        grid=(res.shape[0],),
        in_specs=specs,
        out_specs=out_specs,
        out_shape=outs,
        scratch_shapes=[pltpu.VMEM((rows, width), F32)],
        compiler_params=pltpu.CompilerParams(vmem_limit_bytes=40 * MIB),
        name="guess_windows",
    )(*ops)


def step_call(blk, guess, inv, border, group):
    rows, width = group.shape
    field = by_scenario(guess.shape)
    full = jax.ShapeDtypeStruct(guess.shape, F32)
    return pl.pallas_call(
        functools.partial(step_kernel, guess.shape[2]),
        grid=(guess.shape[0],),
        in_specs=[SMEM, field, by_scenario(inv.shape), by_scenario(border.shape), fixed(group.shape)],
        out_specs=[field, field, fixed((rows, width))],
        out_shape=[full, full, jax.ShapeDtypeStruct((rows, width), F32)],
        compiler_params=pltpu.CompilerParams(vmem_limit_bytes=40 * MIB),
        name="step_windows",
    )(blk, guess, inv, border, group)


def greet(n_s, n_f):
    me_s, me_f = lax.axis_index("scen"), lax.axis_index("fs")
    barrier = pltpu.get_barrier_semaphore()
    for k in range(1, n_s):
        peer = lax.rem(me_s + k, n_s)
        pl.semaphore_signal(barrier, inc=1, device_id=(peer, me_f), device_id_type=MESH)
    for k in range(1, n_f):
        peer = lax.rem(me_f + k, n_f)
        pl.semaphore_signal(barrier, inc=1, device_id=(me_s, peer), device_id_type=MESH)
    pl.semaphore_wait(barrier, n_s + n_f - 2)


def remote(src, dst, send, recv, device):
    return pltpu.make_async_remote_copy(
        src_ref=src, dst_ref=dst, send_sem=send, recv_sem=recv, device_id=device, device_id_type=MESH
    )


def solve_kernel(
    n_s, n_f, part, first, schur, owned, group,
    mats, arrived, rhs, acc, partial, sums, steps,
    load_sem, send1, recv1, send2, recv2, send3, recv3, send4, recv4,
):
    me_s, me_f = lax.axis_index("scen"), lax.axis_index("fs")
    own = first.shape[0]
    aligned = own % 128 == 0
    loads = [pltpu.make_async_copy(schur.at[g], mats.at[g], load_sem.at[g]) for g in range(n_f)]
    for load in loads:
        load.start()
    greet(n_s, n_f)
    sends = []
    for k in range(1, n_s):
        p = lax.rem(me_s + k, n_s)
        sends.append(remote(part.at[p], arrived.at[k], send1.at[k], recv1.at[k], (p, me_f)))
        sends[-1].start()
    total = first[...] + part[me_s].astype(F32)
    for k in range(1, n_s):
        sends[k - 1].wait_recv()
        total = total + arrived[k].astype(F32)
    rhs[0] = total.T.astype(BF16)
    spread = []
    for k in range(1, n_f):
        f = lax.rem(me_f + k, n_f)
        spread.append(remote(rhs.at[0], rhs.at[k], send2.at[k], recv2.at[k], (me_s, f)))
        spread[-1].start()
    for load in loads:
        load.wait()

    def shift(p, k):
        return remote(partial.at[p], sums.at[k], send3.at[k], recv3.at[k], (p, me_f))

    for k in range(n_f):
        if k > 0:
            spread[k - 1].wait_recv()
        g = lax.rem(me_f - k + n_f, n_f)
        if aligned:

            @pl.loop(0, n_s)
            def _(i, k=k, g=g):
                p = lax.rem(me_s + 1 + i, n_s)
                columns = pl.ds(pl.multiple_of(p * own, 128), own)
                value = dot(rhs[k], mats[g, :, columns])
                if k > 0:
                    value = value + acc[p]
                if k < n_f - 1:
                    acc[p] = value
                else:
                    partial[p] = value.astype(BF16)

                    @pl.when(i < n_s - 1)
                    def _():
                        shift(p, i + 1).start()

        else:
            value = dot(rhs[k], mats[g])
            if k > 0:
                value = value + jnp.concatenate([acc[p] for p in range(n_s)], axis=1)
            for p in range(n_s):
                piece = value[:, p * own : (p + 1) * own]
                if k < n_f - 1:
                    acc[p] = piece
                else:
                    partial[p] = piece.astype(BF16)
    if not aligned:
        for k in range(1, n_s):
            shift(lax.rem(me_s + k, n_s), k).start()
    total = partial[me_s].astype(F32)
    for k in range(1, n_s):
        shift(lax.rem(me_s + k, n_s), k).wait_recv()
        total = total + sums[k].astype(F32)
    rounded = total.T.astype(BF16)
    owned[...] = rounded.astype(F32)
    steps[me_s] = rounded
    around = []
    for k in range(1, n_s):
        p = lax.rem(me_s + k, n_s)
        around.append(remote(steps.at[me_s], steps.at[me_s], send4.at[k], recv4.at[k], (p, me_f)))
        around[-1].start()
    for k in range(1, n_s):
        sender = lax.rem(me_s - k + n_s, n_s)
        remote(steps.at[sender], steps.at[sender], send4.at[k], recv4.at[k], (sender, me_f)).wait_recv()
    group[...] = steps[...]
    for k in range(1, n_s):
        sends[k - 1].wait_send()
        shift(lax.rem(me_s + k, n_s), k).wait_send()
        around[k - 1].wait_send()
    for k in range(1, n_f):
        spread[k - 1].wait_send()


def solve_call(n_s, n_f, part, first, schur):
    own, width = first.shape
    dma = pltpu.SemaphoreType.DMA
    return pl.pallas_call(
        functools.partial(solve_kernel, n_s, n_f),
        in_specs=[VMEM, VMEM, ANY],
        out_specs=[VMEM, VMEM],
        out_shape=[
            jax.ShapeDtypeStruct((own, width), F32),
            jax.ShapeDtypeStruct((n_s, own, width), BF16),
        ],
        scratch_shapes=[
            pltpu.VMEM(schur.shape, BF16),
            pltpu.VMEM((n_s, own, width), BF16),
            pltpu.VMEM((n_f, width, own), BF16),
            pltpu.VMEM((n_s, width, own), F32),
            pltpu.VMEM((n_s, width, own), BF16),
            pltpu.VMEM((n_s, width, own), BF16),
            pltpu.VMEM((n_s, own, width), BF16),
            dma((n_f,)),
            dma((n_s,)), dma((n_s,)),
            dma((n_f,)), dma((n_f,)),
            dma((n_s,)), dma((n_s,)),
            dma((n_s,)), dma((n_s,)),
        ],
        compiler_params=pltpu.CompilerParams(
            collective_id=0, has_side_effects=True, vmem_limit_bytes=48 * MIB
        ),
        name="schur_solve",
    )(part, first, schur)


def fold(x):
    return x.reshape(x.shape[0] // 8, 8, x.shape[1]).sum(axis=0)


def image_kernel(n_s, n_f, exact, *refs):
    part, first, owned, gain, step, res, coupled, diag, pairs = refs[:9]
    refs = refs[9:]
    if exact:
        image, refs = refs[0], refs[1:]
    (
        scale, first_out,
        arrived, halo, v_step, v_res, v_coupled, v_diag, v_pairs, high, low, along, energy, inner, outer,
        load_sem, send1, recv1, halo_send, halo_recv, send2, recv2, send3, recv3,
    ) = refs
    me_s, me_f = lax.axis_index("scen"), lax.axis_index("fs")
    scens, count, size = v_step.shape[:3]

    def loads(s):
        moves = ((step, v_step), (diag, v_diag), (pairs, v_pairs), (coupled, v_coupled), (res, v_res))
        return [
            pltpu.make_async_copy(src.at[s], dst.at[s], load_sem.at[s, j]) for j, (src, dst) in enumerate(moves)
        ]

    for s in range(scens):
        for load in loads(s):
            load.start()
    greet(n_s, n_f)
    before = remote(step.at[:, 0], halo.at[1], halo_send.at[1], halo_recv.at[1], (me_s, lax.rem(me_f + n_f - 1, n_f)))
    after = remote(
        step.at[:, count - 1], halo.at[0], halo_send.at[0], halo_recv.at[0], (me_s, lax.rem(me_f + 1, n_f))
    )

    @pl.when(me_f > 0)
    def _():
        before.start()

    @pl.when(me_f < n_f - 1)
    def _():
        after.start()

    sends = []
    for k in range(1, n_s):
        p = lax.rem(me_s + k, n_s)
        sends.append(remote(part.at[p], arrived.at[k], send1.at[k], recv1.at[k], (p, me_f)))
        sends[-1].start()
    along[...] = jnp.zeros_like(along)
    energy[...] = jnp.zeros_like(energy)

    def windows(s, chosen):
        products = []
        for w in chosen:
            mat = jnp.concatenate([v_pairs[s, w, 0], v_diag[s, w], v_pairs[s, w, 1]], axis=1)
            right = high[s, w * size : (w + 3) * size]
            if exact:
                mh, ml = split(mat)
                value = dot(mh, right) + dot(ml, right) + dot(mh, low[s, w * size : (w + 3) * size])
            else:
                value = dot(mat.astype(BF16), right)
            products.append(value)
        a, e = along[...], energy[...]
        for w, value in zip(chosen, products):
            value = value + v_coupled[s, w]
            if exact:
                image[s, w] = value
            a = a + fold(v_res[s, w] * value)
            e = e + fold(value * value)
        along[...] = a
        energy[...] = e

    def place(s, w, value):
        hi, lo = split(value)
        high[s, w * size : (w + 1) * size] = hi
        if exact:
            low[s, w * size : (w + 1) * size] = lo

    @pl.loop(0, scens)
    def _(s):
        for load in loads(s):
            load.wait()
        for w in range(count):
            place(s, w + 1, v_step[s, w])
        windows(s, range(1, count - 1))

    @pl.when(me_f < n_f - 1)
    def _():
        before.wait_recv()

    @pl.when(me_f > 0)
    def _():
        after.wait_recv()

    @pl.when(me_f == n_f - 1)
    def _():
        halo[1] = jnp.zeros(halo.shape[1:], F32)

    @pl.when(me_f == 0)
    def _():
        halo[0] = jnp.zeros(halo.shape[1:], F32)

    @pl.loop(0, scens)
    def _(s):
        place(s, 0, halo[0, s])
        place(s, count + 1, halo[1, s])
        windows(s, (0, count - 1))

    total = part[me_s]
    for k in range(1, n_s):
        sends[k - 1].wait_recv()
        total = total + arrived[k]
    value = gain[...] * owned[...] - total
    a = along[...] + fold(first[...] * value)
    e = energy[...] + fold(value * value)
    inner[0, 0:8] = a
    inner[0, 8:16] = e
    shares = []
    for k in range(1, n_s):
        p = lax.rem(me_s + k, n_s)
        shares.append(remote(inner.at[0], inner.at[k], send2.at[k], recv2.at[k], (p, me_f)))
        shares[-1].start()
    sums = inner[0]
    for k in range(1, n_s):
        shares[k - 1].wait_recv()
        sums = sums + inner[k]
    outer[0] = sums
    lines = []
    for k in range(1, n_f):
        f = lax.rem(me_f + k, n_f)
        lines.append(remote(outer.at[0], outer.at[k], send3.at[k], recv3.at[k], (me_s, f)))
        lines[-1].start()
    for k in range(1, n_f):
        lines[k - 1].wait_recv()
        sums = sums + outer[k]
    a = jnp.sum(sums[0:8], axis=0, keepdims=True)
    e = jnp.sum(sums[8:16], axis=0, keepdims=True)
    ratio = a / (e + 1e-06)
    scale[...] = ratio
    first_out[...] = first[...] - ratio * value

    @pl.when(me_f > 0)
    def _():
        before.wait_send()

    @pl.when(me_f < n_f - 1)
    def _():
        after.wait_send()

    for k in range(1, n_s):
        sends[k - 1].wait_send()
        shares[k - 1].wait_send()
    for k in range(1, n_f):
        lines[k - 1].wait_send()


def image_call(n_s, n_f, exact, part, first, owned, gain, step, res, coupled, diag, pairs):
    own, width = first.shape
    scens, count, size = step.shape[:3]
    dma = pltpu.SemaphoreType.DMA
    outs = [jax.ShapeDtypeStruct((1, width), F32), jax.ShapeDtypeStruct((own, width), F32)]
    if exact:
        outs = [jax.ShapeDtypeStruct(step.shape, F32)] + outs
    padded = (scens, (count + 2) * size, width)
    return pl.pallas_call(
        functools.partial(image_kernel, n_s, n_f, exact),
        in_specs=[VMEM] * 4 + [ANY] * 5,
        out_specs=[VMEM] * len(outs),
        out_shape=outs,
        scratch_shapes=[
            pltpu.VMEM((n_s, own, width), F32),
            pltpu.VMEM((2, scens, size, width), F32),
            pltpu.VMEM(step.shape, F32),
            pltpu.VMEM(res.shape, F32),
            pltpu.VMEM(coupled.shape, F32),
            pltpu.VMEM(diag.shape, F32),
            pltpu.VMEM(pairs.shape, F32),
            pltpu.VMEM(padded, BF16),
            pltpu.VMEM(padded if exact else (1, 16, width), BF16),
            pltpu.VMEM((8, width), F32),
            pltpu.VMEM((8, width), F32),
            pltpu.VMEM((n_s, 16, width), F32),
            pltpu.VMEM((n_f, 16, width), F32),
            dma((scens, 5)),
            dma((n_s,)), dma((n_s,)),
            dma((2,)), dma((2,)),
            dma((n_s,)), dma((n_s,)),
            dma((n_f,)), dma((n_f,)),
        ],
        compiler_params=pltpu.CompilerParams(
            collective_id=1 if exact else 2, has_side_effects=True, vmem_limit_bytes=56 * MIB
        ),
        name="image_exact" if exact else "image_sums",
    )(part, first, owned, gain, step, res, coupled, diag, pairs)


def per_device(
    n_s,
    n_f,
    scen_rhs,
    first_rhs,
    diag_blocks,
    diag_inverse,
    couplings,
    border,
    border_block,
    first_diag,
    schur_inverse,
):
    group_rows = schur_inverse.shape[-1]
    own_rows = first_rhs.shape[1]
    width = scen_rhs.shape[-1]
    schur = schur_inverse.reshape(n_f, own_rows, group_rows)
    gain = first_diag.reshape(own_rows, 1)
    scen_res = scen_rhs
    first_res = first_rhs.reshape(own_rows, width)
    image = scale = scen_sol = first_sol = None
    for round_index in range(ROUNDS):
        if round_index == 0:
            guess, part = guess_call(border_block, scen_res, diag_inverse, border, group_rows)
        else:
            scen_res, guess, part = guess_call(
                border_block, scen_res, diag_inverse, border, group_rows, image, scale
            )
        owned, group = solve_call(n_s, n_f, part.reshape(n_s, own_rows, width), first_res, schur)
        step, coupled, part = step_call(
            border_block, guess, diag_inverse, border, group.reshape(group_rows, width)
        )
        last = round_index == ROUNDS - 1
        found = image_call(
            n_s, n_f, not last, part.reshape(n_s, own_rows, width), first_res, owned, gain,
            step, scen_res, coupled, diag_blocks, couplings,
        )
        if not last:
            image = found[0]
        scale, first_res = found[-2:]
        scen_sol = scale * step if scen_sol is None else scen_sol + scale * step
        first_sol = scale * owned if first_sol is None else first_sol + scale * owned
    return (
        scen_sol,
        first_sol.reshape(1, own_rows, width),
        first_res.reshape(1, own_rows, width),
    )


def solution(mesh):
    return jax.shard_map(
        functools.partial(per_device, mesh.shape["scen"], mesh.shape["fs"]),
        mesh=mesh,
        in_specs=(
            P("scen", "fs", None, None),
            P("fs", "scen", None),
            P("scen", "fs", None, None),
            P("scen", "fs", None, None),
            P("scen", "fs", None, None, None),
            P("scen", "fs", None, None),
            P("scen", "fs"),
            P("fs", "scen"),
            P(None, "scen", "fs", None),
        ),
        out_specs=(P("scen", "fs", None, None), P("fs", "scen", None), P("fs", "scen", None)),
        check_vma=False,
    )
```

time: 584 us -> 263 us (0.45); the launches traced: 575 us -> 262 us
  Pallas kernels: 0 us -> 230 us
  waiting for transfers between devices: 218 us -> 0 us
  matrix products: 162 us -> 0 us
  blocking collectives: 110 us -> 0 us
  local copies, waits for them, and re-layouts: 46.1 us -> 24.6 us
  between operations: 14.9 us -> 0.83 us
  starting transfers between devices: 11.7 us -> 0 us
  other arithmetic: 12.5 us -> 6.48 us
    pallas_call x0 -> x8, Pallas kernels: none -> 230 us  [the longest x2 105 us: solve_call(): pl.pallas_call(functools.partial(solve_kernel, n_s, n_f), in_specs=[VMEM,...]
    dot_general x24 -> x0, matrix products: 162 us -> none  [the longest x8 76.5 us: tile_product(): return jnp.einsum('swij,swjr->swir', mats, values, precision=EXACT)]
    psum x2 -> x0, waiting for transfers between devices: 125 us -> none  [per_device(): summed = lax.psum(solve_partial_value, 'scen')]
    reduce_scatter x4 -> x0, waiting for transfers between devices: 93.1 us -> none  [collect(): lax.psum_scatter(partial_value, 'scen', scatter_dimension=0, tiled=True)]
    psum x2 -> x0, blocking collectives: 78.8 us -> none  [per_device(): along, energy = lax.psum((along, energy), ('scen', 'fs'))]
    all_gather x2 -> x0, blocking collectives: 31.3 us -> none  [per_device(): lax.all_gather(operand, 'fs', axis=0, tiled=True)]
    reshape x10 -> x1, local copies, waits for them, and re-layouts: 28.8 us -> 1.54 us  [per_device(): gain = first_diag.reshape(own_rows, 1)]
    unnamed x43 -> x51, local copies, waits for them, and re-layouts: 9.51 us -> 23.1 us
  transfers between devices with their start and end apart: 10 -> 0, of which waited for: 6 -> 0; matrix products, arithmetic and copies ran while one was open for 13% -> 0% of each run, Pallas kernels for 0% -> 0%
where the time goes in v1:
time: 263 us; the launch traced here: 262 us
  Pallas kernels  230 us (87%)
  local copies, waits for them, and re-layouts  24.6 us (9%)
  other arithmetic  6.48 us (2%)
    pallas_call x2, Pallas kernels, solve_call(): pl.pallas_call(functools.partial(solve_kernel, n_s, n_f), in_specs=[VMEM,...  105 us
    pallas_call x2, Pallas kernels, image_call(): pl.pallas_call(functools.partial(image_kernel, n_s, n_f, exact), in_specs...  81 us
    pallas_call x2, Pallas kernels, step_call(): pl.pallas_call(functools.partial(step_kernel, guess.shape[2]), grid=(gues...  29.5 us
    unnamed x51, local copies, waits for them, and re-layouts  23.1 us
    pallas_call x2, Pallas kernels, guess_call(): pl.pallas_call(functools.partial(guess_kernel, update, size), grid=(res.s...  14.8 us
    add x1, other arithmetic, per_device(): scen_sol = scale * step if scen_sol is None else scen_sol + scale * step  5.74 us

profile of v1, /device:TPU:0, one launch (start us, length us, event | category | flops | bytes accessed | tf_op | source)
XLA Modules:
  0.0 262.3 jit_solution(17104068403574535504)
XLA Ops:
  0.6 1.5 copy.12.refs_3_
  2.2 2.2 copy-done
  4.4 1.6 copy-done.1
  5.9 0.7 copy-done.19
  6.6 6.6 %guess_windows.2 = (f32[8,16,64,128]{3,2,1,0:T(8,128)S(1)}, bf16[4096,128]{1,0:T(8,128)(2,1)S(1)}) custom-call(s32[8,16]{1,0:T(8,128)S(1)} %copy-done.19, f32[8,16,64,128]{3,2,1,0:T(8,128)S(1)} %copy-done, bf16[8,16,64,64]{3,2,1,0:T(8,128)(2,1)S(1)} %copy-done.1, f32[8,16,64,64]{3,2,1,0:T(8,128)} %border.3), custom_call_target="tpu_custom_call" | custom-call | tf_op jit(solution)/shard_map/guess_windows/pallas_call | solution.py:117
  13.2 0.0 copy-start.7
  13.3 2.0 copy-done.7
  15.3 0.0 copy-done.13
  15.3 54.3 %schur_solve.2 = (f32[512,128]{1,0:T(8,128)S(1)}, bf16[8,512,128]{2,1,0:T(8,128)(2,1)S(1)}) custom-call(bf16[8,512,128]{2,1,0:T(8,128)(2,1)S(1)} %bitcast.19, f32[512,128]{1,0:T(8,128)S(1)} %bitcast.17, bf16[4,512,4096]{2,1,0:T(8,128)(2,1)} %bitcast.24), custom_call_target="tpu_custom_call" | custom-call | tf_op jit(solution)/shard_map/schur_solve/pallas_call | solution.py:257
  69.6 0.0 copy-start.15
  69.6 0.7 copy-done.15
  70.3 0.0 copy-done.2
  70.3 0.0 copy-done.20
  70.3 14.7 %step_windows.2 = (f32[8,16,64,128]{3,2,1,0:T(8,128)S(1)}, f32[8,16,64,128]{3,2,1,0:T(8,128)S(1)}, f32[4096,128]{1,0:T(8,128)S(1)}) custom-call(s32[8,16]{1,0:T(8,128)S(1)} %copy-done.20, f32[8,16,64,128]{3,2,1,0:T(8,128)} %copy-done.7, bf16[8,16,64,64]{3,2,1,0:T(8,128)(2,1)S(1)} %copy-done.2, f32[8,16,64,64]{3,2,1,0:T(8,128)} %border.3, ...), custom_call_target="tpu_custom_call" | custom-call | tf_op jit(solution)/shard_map/step_windows/pallas_call | solution.py:133
  85.0 0.0 copy-start.3
  85.0 2.0 copy-done.3
  87.0 2.0 copy-done.10
  89.0 1.4 copy-done.12
  90.4 40.9 %image_exact.1 = (f32[8,16,64,128]{3,2,1,0:T(8,128)}, f32[1,128]{1,0:T(1,128)}, f32[512,128]{1,0:T(8,128)}) custom-call(f32[8,512,128]{2,1,0:T(8,128)} %bitcast.15, f32[512,128]{1,0:T(8,128)} %bitcast.16, f32[512,128]{1,0:T(8,128)} %copy-done.15, f32[512,1]{1,0:T(8,128)} %copy.12.refs_3_, f32[8,16,64,128]{3,2,1,0:T(8,128)} %copy-done.3, ...), custom_call_target="tpu_custom_call" | custom-call | tf_op jit(solution)/shard_map/image_exact/pallas_call | solution.py:447
  131.2 0.0 copy-start.21
  131.2 0.6 copy-done.21
  131.8 8.2 %guess_windows.3 = (f32[8,16,64,128]{3,2,1,0:T(8,128)S(1)}, f32[8,16,64,128]{3,2,1,0:T(8,128)S(1)}, bf16[4096,128]{1,0:T(8,128)(2,1)S(1)}) custom-call(s32[8,16]{1,0:T(8,128)S(1)} %copy-done.20, f32[8,16,64,128]{3,2,1,0:T(8,128)} %refs_1_.3, f32[8,16,64,128]{3,2,1,0:T(8,128)} %get-tuple-element.31.refs_2_, f32[1,128]{1,0:T(1,128)S(1)} %copy-done.21, ...), custom_call_target="tpu_custom_call" | custom-call | tf_op jit(solution)/shard_map/guess_windows/pallas_call | solution.py:117
  140.0 0.0 copy-start.6
  140.0 2.0 copy-done.6
  142.0 2.0 copy-done.8
  144.0 0.0 copy-done.14
  144.0 50.9 %schur_solve.3 = (f32[512,128]{1,0:T(8,128)S(1)}, bf16[8,512,128]{2,1,0:T(8,128)(2,1)S(1)}) custom-call(bf16[8,512,128]{2,1,0:T(8,128)(2,1)S(1)} %bitcast.18, f32[512,128]{1,0:T(8,128)S(1)} %copy-done.14, bf16[4,512,4096]{2,1,0:T(8,128)(2,1)} %bitcast.25), custom_call_target="tpu_custom_call" | custom-call | tf_op jit(solution)/shard_map/schur_solve/pallas_call | solution.py:257
  194.9 0.0 copy-start.17
  194.9 14.8 %step_windows.3 = (f32[8,16,64,128]{3,2,1,0:T(8,128)S(1)}, f32[8,16,64,128]{3,2,1,0:T(8,128)S(1)}, f32[4096,128]{1,0:T(8,128)S(1)}) custom-call(s32[8,16]{1,0:T(8,128)S(1)} %copy-done.20, f32[8,16,64,128]{3,2,1,0:T(8,128)} %copy-done.6, bf16[8,16,64,64]{3,2,1,0:T(8,128)(2,1)S(1)} %copy-done.2, f32[8,16,64,64]{3,2,1,0:T(8,128)} %border.3, ...), custom_call_target="tpu_custom_call" | custom-call | tf_op jit(solution)/shard_map/step_windows/pallas_call | solution.py:133
  209.7 0.0 copy-done.17
  209.7 0.0 copy-start.5
  209.7 2.0 copy-done.5
  211.6 2.0 copy-done.9
  213.6 1.3 copy-done.11
  214.9 40.1 %image_sums.1 = (f32[1,128]{1,0:T(1,128)}, f32[512,128]{1,0:T(8,128)}) custom-call(f32[8,512,128]{2,1,0:T(8,128)} %bitcast.14, f32[512,128]{1,0:T(8,128)} %get-tuple-element.34.first.refs_1_, f32[512,128]{1,0:T(8,128)} %copy-done.17, f32[512,1]{1,0:T(8,128)} %copy.12.refs_3_, f32[8,16,64,128]{3,2,1,0:T(8,128)} %copy-done.5, f32[8,16,64,128]{3,2,1,0:T(8,128)} %copy-done.8, ...), custom_call_target="tpu_custom_call" | custom-call | tf_op jit(solution)/shard_map/image_sums/pallas_call | solution.py:447
  255.1 0.0 copy-done.4
  255.1 0.0 copy-done.22
  255.1 0.0 copy-start.16
  255.1 0.0 copy-start.18
  255.1 0.0 copy-start.24
  255.1 0.0 copy-start.23
  255.1 5.7 %multiply_add_fusion = f32[8,16,64,128]{3,2,1,0:T(8,128)} fusion(f32[8,16,64,128]{3,2,1,0:T(8,128)} %copy-done.5, f32[8,16,64,128]{3,2,1,0:T(8,128)S(1)} %copy-done.4, f32[128]{0:T(128)} %bitcast.28, f32[128]{0:T(128)S(1)} %bitcast.22), kind=kLoop, calls=%fused_computation | loop fusion | flops 3145728 | bytes 12583936 | tf_op jit(solution)/shard_map/add | solution.py:519
  260.9 0.0 copy-done.16
  260.9 0.0 copy-done.18
  260.9 0.0 copy-done.24
  260.9 0.7 add_bitcast_fusion
  261.6 0.0 copy-done.23
  261.6 0.7 copy.15
  (14 shorter events, 0.0 us)
Async XLA Ops:
  2.2 2.2 copy-start
  4.4 1.6 copy-start.1
  5.9 0.7 copy-start.19
  6.6 8.6 %copy-start.13 = (f32[1,512,128]{2,1,0:T(8,128)S(1)}, f32[1,512,128]{2,1,0:T(8,128)}, u32[]{:S(2)}) copy-start(f32[1,512,128]{2,1,0:T(8,128)} %param.10) | copy-start | bytes 786436
  13.2 2.0 copy-start.7
  15.3 55.1 %copy-start.2 = (bf16[8,16,64,64]{3,2,1,0:T(8,128)(2,1)S(1)}, bf16[8,16,64,64]{3,2,1,0:T(8,128)(2,1)}, u32[]{:S(2)}) copy-start(bf16[8,16,64,64]{3,2,1,0:T(8,128)(2,1)} %inv.3) | copy-start | bytes 3145732
  15.3 55.1 %copy-start.20 = (s32[8,16]{1,0:T(8,128)S(1)}, s32[8,16]{1,0:T(8,128)}, u32[]{:S(2)}) copy-start(s32[8,16]{1,0:T(8,128)} %blk.3) | copy-start | bytes 1540
  69.6 0.7 copy-start.15
  85.0 2.0 copy-start.3
  87.0 2.0 copy-start.10
  89.0 1.4 copy-start.12
  131.2 0.6 copy-start.21
  131.8 12.2 %copy-start.14 = (f32[512,128]{1,0:T(8,128)S(1)}, f32[512,128]{1,0:T(8,128)}, u32[]{:S(2)}) copy-start(f32[512,128]{1,0:T(8,128)} %get-tuple-element.34.first.refs_1_) | copy-start | bytes 786436
  140.0 2.0 copy-start.6
  141.9 2.0 copy-start.8
  194.9 14.8 %copy-start.17 = (f32[512,128]{1,0:T(8,128)}, f32[512,128]{1,0:T(8,128)S(1)}, u32[]{:S(2)}) copy-start(f32[512,128]{1,0:T(8,128)S(1)} %get-tuple-element.37.refs_2_) | copy-start | bytes 786436
  209.7 2.0 copy-start.5
  211.6 2.0 copy-start.9
  213.6 1.3 copy-start.11
  214.9 40.1 %copy-start.4 = (f32[8,16,64,128]{3,2,1,0:T(8,128)S(1)}, f32[8,16,64,128]{3,2,1,0:T(8,128)}, u32[]{:S(2)}) copy-start(f32[8,16,64,128]{3,2,1,0:T(8,128)} %copy-done.3) | copy-start | bytes 12582916
  214.9 40.1 %copy-start.22 = (f32[1,128]{1,0:T(1,128)S(1)}, f32[1,128]{1,0:T(1,128)}, u32[]{:S(2)}) copy-start(f32[1,128]{1,0:T(1,128)} %get-tuple-element.30.refs_3_) | copy-start | bytes 1540
  255.1 5.8 %copy-start.16 = (f32[512,128]{1,0:T(8,128)S(1)}, f32[512,128]{1,0:T(8,128)}, u32[]{:S(2)}) copy-start(f32[512,128]{1,0:T(8,128)} %copy-done.15) | copy-start | bytes 786436
  255.1 5.8 %copy-start.18 = (f32[512,128]{1,0:T(8,128)S(1)}, f32[512,128]{1,0:T(8,128)}, u32[]{:S(2)}) copy-start(f32[512,128]{1,0:T(8,128)} %copy-done.17) | copy-start | bytes 786436
  255.1 5.8 %copy-start.24 = (f32[1,128]{1,0:T(1,128)S(1)}, f32[1,128]{1,0:T(1,128)}, u32[]{:S(2)}) copy-start(f32[1,128]{1,0:T(1,128)} %get-tuple-element.41) | copy-start | bytes 1540
  255.1 6.5 %copy-start.23 = (f32[512,128]{1,0:T(8,128)S(1)}, f32[512,128]{1,0:T(8,128)}, u32[]{:S(2)}) copy-start(f32[512,128]{1,0:T(8,128)} %get-tuple-element.42) | copy-start | bytes 786436

commit v2 on v1

--- a/solution.py
+++ b/solution.py
@@ -8,10 +8,11 @@
 from jax.sharding import PartitionSpec as P
 
 ROUNDS = 2
-MIB = 1024 * 1024
+LIMIT = 60 * 1024 * 1024
 MESH = pl.DeviceIdType.MESH
 F32 = jnp.float32
 BF16 = jnp.bfloat16
+FAR = jnp.bfloat16
 VMEM = pl.BlockSpec(memory_space=pltpu.VMEM)
 ANY = pl.BlockSpec(memory_space=pl.ANY)
 
@@ -121,7 +122,7 @@
         out_specs=out_specs,
         out_shape=outs,
         scratch_shapes=[pltpu.VMEM((rows, width), F32)],
-        compiler_params=pltpu.CompilerParams(vmem_limit_bytes=40 * MIB),
+        compiler_params=pltpu.CompilerParams(vmem_limit_bytes=LIMIT),
         name="guess_windows",
     )(*ops)
 
@@ -136,21 +137,16 @@
         in_specs=[SMEM, field, by_scenario(inv.shape), by_scenario(border.shape), fixed(group.shape)],
         out_specs=[field, field, fixed((rows, width))],
         out_shape=[full, full, jax.ShapeDtypeStruct((rows, width), F32)],
-        compiler_params=pltpu.CompilerParams(vmem_limit_bytes=40 * MIB),
+        compiler_params=pltpu.CompilerParams(vmem_limit_bytes=LIMIT),
         name="step_windows",
     )(blk, guess, inv, border, group)
 
 
-def greet(n_s, n_f):
-    me_s, me_f = lax.axis_index("scen"), lax.axis_index("fs")
+def greet(devices):
     barrier = pltpu.get_barrier_semaphore()
-    for k in range(1, n_s):
-        peer = lax.rem(me_s + k, n_s)
-        pl.semaphore_signal(barrier, inc=1, device_id=(peer, me_f), device_id_type=MESH)
-    for k in range(1, n_f):
-        peer = lax.rem(me_f + k, n_f)
-        pl.semaphore_signal(barrier, inc=1, device_id=(me_s, peer), device_id_type=MESH)
-    pl.semaphore_wait(barrier, n_s + n_f - 2)
+    for device in devices:
+        pl.semaphore_signal(barrier, inc=1, device_id=device, device_id_type=MESH)
+    pl.semaphore_wait(barrier, len(devices))
 
 
 def remote(src, dst, send, recv, device):
@@ -159,100 +155,163 @@
     )
 
 
+class Places:
+    def __init__(self, n_s, n_f):
+        self.n_s, self.n_f, self.chips = n_s, n_f, n_s // 2
+        self.me_s, self.me_f = lax.axis_index("scen"), lax.axis_index("fs")
+        self.chip, self.core = self.me_s // 2, self.me_s % 2
+        self.sibling = (self.chip * 2 + 1 - self.core, self.me_f)
+
+    def ahead(self, k):
+        return lax.rem(self.chip + k, self.chips)
+
+    def behind(self, k):
+        return lax.rem(self.chip - k + self.chips, self.chips)
+
+    def peer(self, k):
+        return (self.ahead(k) * 2 + self.core, self.me_f)
+
+    def along(self, k):
+        return (self.me_s, lax.rem(self.me_f + k, self.n_f))
+
+    def greeted(self):
+        near = [self.sibling] + [self.peer(k) for k in range(1, self.chips)]
+        return near + [self.along(k) for k in range(1, self.n_f)]
+
+
+class Scatter:
+    def __init__(self, at, part, pair, mixed, arrived, sems):
+        self.at, self.part, self.pair, self.mixed, self.arrived = at, part, pair, mixed, arrived
+        near_send, near_recv, far_send, far_recv = sems
+        self.near = remote(part.at[:, 1 - at.core], pair, near_send.at[0], near_recv.at[0], at.sibling)
+        self.far = [
+            remote(mixed.at[k], arrived.at[k], far_send.at[k], far_recv.at[k], at.peer(k))
+            for k in range(1, at.chips)
+        ]
+
+    def mix(self, chip):
+        return self.part[chip, self.at.core].astype(F32) + self.pair[chip].astype(F32)
+
+    def pass_on(self):
+        self.near.wait_recv()
+        for k, far in enumerate(self.far, 1):
+            self.mixed[k] = self.mix(self.at.ahead(k)).astype(self.mixed.dtype)
+            far.start()
+
+    def total(self):
+        value = self.mix(self.at.chip)
+        for k, far in enumerate(self.far, 1):
+            far.wait_recv()
+            value = value + self.arrived[k].astype(F32)
+        return value
+
+    def finish(self):
+        self.near.wait_send()
+        for far in self.far:
+            far.wait_send()
+
+
 def solve_kernel(
     n_s, n_f, part, first, schur, owned, group,
-    mats, arrived, rhs, acc, partial, sums, steps,
-    load_sem, send1, recv1, send2, recv2, send3, recv3, send4, recv4,
+    mats, pair1, mixed1, arrived1, rhs, acc, partial, pair2, mixed2, arrived2, steps,
+    load_sem, a1, b1, c1, d1, line_send, line_recv, a2, b2, c2, d2, far_send, far_recv, near_send, near_recv,
 ):
-    me_s, me_f = lax.axis_index("scen"), lax.axis_index("fs")
+    at = Places(n_s, n_f)
+    me_f, core, chips = at.me_f, at.core, at.chips
     own = first.shape[0]
     aligned = own % 128 == 0
     loads = [pltpu.make_async_copy(schur.at[g], mats.at[g], load_sem.at[g]) for g in range(n_f)]
     for load in loads:
         load.start()
-    greet(n_s, n_f)
-    sends = []
-    for k in range(1, n_s):
-        p = lax.rem(me_s + k, n_s)
-        sends.append(remote(part.at[p], arrived.at[k], send1.at[k], recv1.at[k], (p, me_f)))
-        sends[-1].start()
-    total = first[...] + part[me_s].astype(F32)
-    for k in range(1, n_s):
-        sends[k - 1].wait_recv()
-        total = total + arrived[k].astype(F32)
-    rhs[0] = total.T.astype(BF16)
-    spread = []
-    for k in range(1, n_f):
-        f = lax.rem(me_f + k, n_f)
-        spread.append(remote(rhs.at[0], rhs.at[k], send2.at[k], recv2.at[k], (me_s, f)))
-        spread[-1].start()
+    greet(at.greeted())
+    one = Scatter(at, part, pair1, mixed1, arrived1, (a1, b1, c1, d1))
+    two = Scatter(at, partial, pair2, mixed2, arrived2, (a2, b2, c2, d2))
+    one.near.start()
+    one.pass_on()
+    rhs[me_f] = (first[...] + one.total()).T.astype(BF16)
+
+    def hop(t, way):
+        g = lax.rem(me_f + (t if way else n_f - t), n_f)
+        copy = functools.partial(
+            remote, rhs.at[g], rhs.at[g], line_send.at[way, t], line_recv.at[way, t + 1], at.along(n_f - 1 if way else 1)
+        )
+        has = (me_f + t < n_f) if way else (me_f - t >= 0)
+        more = (me_f > 0) if way else (me_f < n_f - 1)
+        return copy, has, jnp.logical_and(has, more), g
+
+    def send(t):
+        for way in range(2):
+            copy, has, goes, g = hop(t, way)
+            if t > 0:
+                arrival = remote(
+                    rhs.at[g], rhs.at[g], line_send.at[way, t], line_recv.at[way, t], at.along(1)
+                )
+                pl.when(has)(arrival.wait_recv)
+            if t < n_f - 1:
+                pl.when(goes)(lambda copy=copy: copy().start())
+
+    def multiply(g, begin):
+        if aligned:
+
+            @pl.loop(0, n_s)
+            def _(p):
+                columns = pl.ds(pl.multiple_of(p * own, 128), own)
+                value = dot(rhs[g], mats[g, :, columns])
+                acc[p] = value if begin else acc[p] + value
+
+        else:
+            value = dot(rhs[g], mats[g])
+            for p in range(n_s):
+                piece = value[:, p * own : (p + 1) * own]
+                acc[p] = piece if begin else acc[p] + piece
+
+    send(0)
     for load in loads:
         load.wait()
-
-    def shift(p, k):
-        return remote(partial.at[p], sums.at[k], send3.at[k], recv3.at[k], (p, me_f))
-
-    for k in range(n_f):
-        if k > 0:
-            spread[k - 1].wait_recv()
-        g = lax.rem(me_f - k + n_f, n_f)
-        if aligned:
-
-            @pl.loop(0, n_s)
-            def _(i, k=k, g=g):
-                p = lax.rem(me_s + 1 + i, n_s)
-                columns = pl.ds(pl.multiple_of(p * own, 128), own)
-                value = dot(rhs[k], mats[g, :, columns])
-                if k > 0:
-                    value = value + acc[p]
-                if k < n_f - 1:
-                    acc[p] = value
-                else:
-                    partial[p] = value.astype(BF16)
-
-                    @pl.when(i < n_s - 1)
-                    def _():
-                        shift(p, i + 1).start()
-
-        else:
-            value = dot(rhs[k], mats[g])
-            if k > 0:
-                value = value + jnp.concatenate([acc[p] for p in range(n_s)], axis=1)
-            for p in range(n_s):
-                piece = value[:, p * own : (p + 1) * own]
-                if k < n_f - 1:
-                    acc[p] = piece
-                else:
-                    partial[p] = piece.astype(BF16)
-    if not aligned:
-        for k in range(1, n_s):
-            shift(lax.rem(me_s + k, n_s), k).start()
-    total = partial[me_s].astype(F32)
-    for k in range(1, n_s):
-        shift(lax.rem(me_s + k, n_s), k).wait_recv()
-        total = total + sums[k].astype(F32)
-    rounded = total.T.astype(BF16)
+    multiply(me_f, True)
+    for t in range(1, n_f):
+        send(t)
+        for way in range(2):
+            _, has, _, g = hop(t, way)
+            pl.when(has)(functools.partial(multiply, g, False))
+    for q in range(chips):
+        partial[q, 1 - core] = acc[2 * q + 1 - core].astype(BF16)
+    two.near.start()
+    for q in range(chips):
+        partial[q, core] = acc[2 * q + core].astype(BF16)
+    two.pass_on()
+    rounded = two.total().T.astype(BF16)
+    steps[at.chip, core] = rounded
+
+    mine = steps.at[at.chip, core]
+    across = [remote(mine, mine, far_send.at[k], far_recv.at[k], at.peer(k)) for k in range(1, chips)]
+    for copy in across:
+        copy.start()
+    over = [remote(mine, mine, near_send.at[0], near_recv.at[0], at.sibling)]
+    over[0].start()
     owned[...] = rounded.astype(F32)
-    steps[me_s] = rounded
-    around = []
-    for k in range(1, n_s):
-        p = lax.rem(me_s + k, n_s)
-        around.append(remote(steps.at[me_s], steps.at[me_s], send4.at[k], recv4.at[k], (p, me_f)))
-        around[-1].start()
-    for k in range(1, n_s):
-        sender = lax.rem(me_s - k + n_s, n_s)
-        remote(steps.at[sender], steps.at[sender], send4.at[k], recv4.at[k], (sender, me_f)).wait_recv()
+    for k in range(1, chips):
+        spot = steps.at[at.behind(k), core]
+        remote(spot, spot, far_send.at[k], far_recv.at[k], at.sibling).wait_recv()
+        over.append(remote(spot, spot, near_send.at[k], near_recv.at[k], at.sibling))
+        over[-1].start()
+    for k in range(chips):
+        spot = steps.at[at.behind(k), 1 - core]
+        remote(spot, spot, near_send.at[k], near_recv.at[k], at.sibling).wait_recv()
     group[...] = steps[...]
-    for k in range(1, n_s):
-        sends[k - 1].wait_send()
-        shift(lax.rem(me_s + k, n_s), k).wait_send()
-        around[k - 1].wait_send()
-    for k in range(1, n_f):
-        spread[k - 1].wait_send()
+    one.finish()
+    two.finish()
+    for copy in across + over:
+        copy.wait_send()
+    for t in range(n_f - 1):
+        for way in range(2):
+            copy, _, goes, _ = hop(t, way)
+            pl.when(goes)(lambda copy=copy: copy().wait_send())
 
 
 def solve_call(n_s, n_f, part, first, schur):
     own, width = first.shape
+    chips = n_s // 2
     dma = pltpu.SemaphoreType.DMA
     return pl.pallas_call(
         functools.partial(solve_kernel, n_s, n_f),
@@ -260,24 +319,28 @@
         out_specs=[VMEM, VMEM],
         out_shape=[
             jax.ShapeDtypeStruct((own, width), F32),
-            jax.ShapeDtypeStruct((n_s, own, width), BF16),
+            jax.ShapeDtypeStruct(part.shape, BF16),
         ],
         scratch_shapes=[
             pltpu.VMEM(schur.shape, BF16),
-            pltpu.VMEM((n_s, own, width), BF16),
+            pltpu.VMEM((chips, own, width), BF16),
+            pltpu.VMEM((chips, own, width), BF16),
+            pltpu.VMEM((chips, own, width), BF16),
             pltpu.VMEM((n_f, width, own), BF16),
             pltpu.VMEM((n_s, width, own), F32),
-            pltpu.VMEM((n_s, width, own), BF16),
-            pltpu.VMEM((n_s, width, own), BF16),
-            pltpu.VMEM((n_s, own, width), BF16),
+            pltpu.VMEM((chips, 2, width, own), BF16),
+            pltpu.VMEM((chips, width, own), BF16),
+            pltpu.VMEM((chips, width, own), BF16),
+            pltpu.VMEM((chips, width, own), BF16),
+            pltpu.VMEM(part.shape, BF16),
             dma((n_f,)),
-            dma((n_s,)), dma((n_s,)),
-            dma((n_f,)), dma((n_f,)),
-            dma((n_s,)), dma((n_s,)),
-            dma((n_s,)), dma((n_s,)),
+            dma((1,)), dma((1,)), dma((chips,)), dma((chips,)),
+            dma((2, n_f)), dma((2, n_f)),
+            dma((1,)), dma((1,)), dma((chips,)), dma((chips,)),
+            dma((chips,)), dma((chips,)), dma((chips,)), dma((chips,)),
         ],
         compiler_params=pltpu.CompilerParams(
-            collective_id=0, has_side_effects=True, vmem_limit_bytes=48 * MIB
+            collective_id=0, has_side_effects=True, vmem_limit_bytes=LIMIT
         ),
         name="schur_solve",
     )(part, first, schur)
@@ -294,10 +357,11 @@
         image, refs = refs[0], refs[1:]
     (
         scale, first_out,
-        arrived, halo, v_step, v_res, v_coupled, v_diag, v_pairs, high, low, along, energy, inner, outer,
-        load_sem, send1, recv1, halo_send, halo_recv, send2, recv2, send3, recv3,
+        pair, mixed, arrived, halo, v_step, v_res, v_coupled, v_diag, v_pairs, high, low, along, energy, inner, outer,
+        load_sem, a1, b1, c1, d1, halo_send, halo_recv, send2, recv2, send3, recv3,
     ) = refs
-    me_s, me_f = lax.axis_index("scen"), lax.axis_index("fs")
+    at = Places(n_s, n_f)
+    me_s, me_f = at.me_s, at.me_f
     scens, count, size = v_step.shape[:3]
 
     def loads(s):
@@ -309,7 +373,10 @@
     for s in range(scens):
         for load in loads(s):
             load.start()
-    greet(n_s, n_f)
+    others = [(lax.rem(me_s + k, n_s), me_f) for k in range(1, n_s)]
+    greet(others + [at.along(k) for k in range(1, n_f)])
+    one = Scatter(at, part, pair, mixed, arrived, (a1, b1, c1, d1))
+    one.near.start()
     before = remote(step.at[:, 0], halo.at[1], halo_send.at[1], halo_recv.at[1], (me_s, lax.rem(me_f + n_f - 1, n_f)))
     after = remote(
         step.at[:, count - 1], halo.at[0], halo_send.at[0], halo_recv.at[0], (me_s, lax.rem(me_f + 1, n_f))
@@ -323,11 +390,6 @@
     def _():
         after.start()
 
-    sends = []
-    for k in range(1, n_s):
-        p = lax.rem(me_s + k, n_s)
-        sends.append(remote(part.at[p], arrived.at[k], send1.at[k], recv1.at[k], (p, me_f)))
-        sends[-1].start()
     along[...] = jnp.zeros_like(along)
     energy[...] = jnp.zeros_like(energy)
 
@@ -358,6 +420,8 @@
         if exact:
             low[s, w * size : (w + 1) * size] = lo
 
+    one.pass_on()
+
     @pl.loop(0, scens)
     def _(s):
         for load in loads(s):
@@ -388,11 +452,7 @@
         place(s, count + 1, halo[1, s])
         windows(s, (0, count - 1))
 
-    total = part[me_s]
-    for k in range(1, n_s):
-        sends[k - 1].wait_recv()
-        total = total + arrived[k]
-    value = gain[...] * owned[...] - total
+    value = gain[...] * owned[...] - one.total()
     a = along[...] + fold(first[...] * value)
     e = energy[...] + fold(value * value)
     inner[0, 0:8] = a
@@ -430,8 +490,8 @@
         after.wait_send()
 
     for k in range(1, n_s):
-        sends[k - 1].wait_send()
         shares[k - 1].wait_send()
+    one.finish()
     for k in range(1, n_f):
         lines[k - 1].wait_send()
 
@@ -439,6 +499,7 @@
 def image_call(n_s, n_f, exact, part, first, owned, gain, step, res, coupled, diag, pairs):
     own, width = first.shape
     scens, count, size = step.shape[:3]
+    chips = n_s // 2
     dma = pltpu.SemaphoreType.DMA
     outs = [jax.ShapeDtypeStruct((1, width), F32), jax.ShapeDtypeStruct((own, width), F32)]
     if exact:
@@ -450,7 +511,9 @@
         out_specs=[VMEM] * len(outs),
         out_shape=outs,
         scratch_shapes=[
-            pltpu.VMEM((n_s, own, width), F32),
+            pltpu.VMEM((chips, own, width), F32),
+            pltpu.VMEM((chips, own, width), FAR),
+            pltpu.VMEM((chips, own, width), FAR),
             pltpu.VMEM((2, scens, size, width), F32),
             pltpu.VMEM(step.shape, F32),
             pltpu.VMEM(res.shape, F32),
@@ -464,13 +527,13 @@
             pltpu.VMEM((n_s, 16, width), F32),
             pltpu.VMEM((n_f, 16, width), F32),
             dma((scens, 5)),
-            dma((n_s,)), dma((n_s,)),
+            dma((1,)), dma((1,)), dma((chips,)), dma((chips,)),
             dma((2,)), dma((2,)),
             dma((n_s,)), dma((n_s,)),
             dma((n_f,)), dma((n_f,)),
         ],
         compiler_params=pltpu.CompilerParams(
-            collective_id=1 if exact else 2, has_side_effects=True, vmem_limit_bytes=56 * MIB
+            collective_id=1 if exact else 2, has_side_effects=True, vmem_limit_bytes=LIMIT
         ),
         name="image_exact" if exact else "image_sums",
     )(part, first, owned, gain, step, res, coupled, diag, pairs)
@@ -504,13 +567,13 @@
             scen_res, guess, part = guess_call(
                 border_block, scen_res, diag_inverse, border, group_rows, image, scale
             )
-        owned, group = solve_call(n_s, n_f, part.reshape(n_s, own_rows, width), first_res, schur)
+        owned, group = solve_call(n_s, n_f, part.reshape(n_s // 2, 2, own_rows, width), first_res, schur)
         step, coupled, part = step_call(
             border_block, guess, diag_inverse, border, group.reshape(group_rows, width)
         )
         last = round_index == ROUNDS - 1
         found = image_call(
-            n_s, n_f, not last, part.reshape(n_s, own_rows, width), first_res, owned, gain,
+            n_s, n_f, not last, part.reshape(n_s // 2, 2, own_rows, width), first_res, owned, gain,
             step, scen_res, coupled, diag_blocks, couplings,
         )
         if not last:

time: 263 us -> 212 us (0.81)
  Pallas kernels: 230 us -> 200 us
  local copies, waits for them, and re-layouts: 24.6 us -> 2.26 us
    pallas_call x2, Pallas kernels: 81 us -> 48.8 us  [image_call(): pl.pallas_call(functools.partial(image_kernel, n_s, n_f, exact), in_specs...]
    unnamed x51 -> x11, local copies, waits for them, and re-layouts: 23.1 us -> 0.72 us
    pallas_call x2, Pallas kernels: 105 us -> 96 us  [solve_call(): pl.pallas_call(functools.partial(solve_kernel, n_s, n_f), in_specs=[VMEM,...]
    pallas_call x2, Pallas kernels: 14.8 us -> 21.8 us  [guess_call(): pl.pallas_call(functools.partial(guess_kernel, update, size), grid=(res.s...]
    pallas_call x2, Pallas kernels: 29.5 us -> 33.7 us  [step_call(): pl.pallas_call(functools.partial(step_kernel, guess.shape[2]), grid=(gues...]
where the time goes in v2:
time: 212 us; the launch traced here: 211 us
  Pallas kernels  200 us (94%)
  other arithmetic  7.74 us (4%)
  local copies, waits for them, and re-layouts  2.26 us (1%)
    pallas_call x2, Pallas kernels, solve_call(): pl.pallas_call(functools.partial(solve_kernel, n_s, n_f), in_specs=[VMEM,...  96 us
    pallas_call x2, Pallas kernels, image_call(): pl.pallas_call(functools.partial(image_kernel, n_s, n_f, exact), in_specs...  48.8 us
    pallas_call x2, Pallas kernels, step_call(): pl.pallas_call(functools.partial(step_kernel, guess.shape[2]), grid=(gues...  33.7 us
    pallas_call x2, Pallas kernels, guess_call(): pl.pallas_call(functools.partial(guess_kernel, update, size), grid=(res.s...  21.8 us
    add x1, other arithmetic, per_device(): scen_sol = scale * step if scen_sol is None else scen_sol + scale * step  7 us

profile of v2, /device:TPU:0, one launch (start us, length us, event | category | flops | bytes accessed | tf_op | source)
XLA Modules:
  0.0 211.1 jit_solution(12422815911241505361)
XLA Ops:
  0.6 1.5 copy.12.refs_3_
  2.2 9.8 %guess_windows.2 = (f32[8,16,64,128]{3,2,1,0:T(8,128)}, bf16[4096,128]{1,0:T(8,128)(2,1)}) custom-call(s32[8,16]{1,0:T(8,128)} %blk.3, f32[8,16,64,128]{3,2,1,0:T(8,128)} %refs_1_.3, bf16[8,16,64,64]{3,2,1,0:T(8,128)(2,1)} %inv.3, f32[8,16,64,64]{3,2,1,0:T(8,128)} %border.3), custom_call_target="tpu_custom_call" | custom-call | tf_op jit(solution)/shard_map/guess_windows/pallas_call | solution.py:118
  11.9 49.6 %schur_solve.2 = (f32[512,128]{1,0:T(8,128)}, bf16[4,2,512,128]{3,2,1,0:T(8,128)(2,1)}) custom-call(bf16[4,2,512,128]{3,2,1,0:T(8,128)(2,1)} %bitcast.21, f32[512,128]{1,0:T(8,128)} %bitcast.18, bf16[4,512,4096]{2,1,0:T(8,128)(2,1)} %bitcast.14), custom_call_target="tpu_custom_call" | custom-call | tf_op jit(solution)/shard_map/schur_solve/pallas_call | solution.py:316
  61.6 16.9 %step_windows.2 = (f32[8,16,64,128]{3,2,1,0:T(8,128)}, f32[8,16,64,128]{3,2,1,0:T(8,128)}, f32[4096,128]{1,0:T(8,128)}) custom-call(s32[8,16]{1,0:T(8,128)} %blk.3, f32[8,16,64,128]{3,2,1,0:T(8,128)} %get-tuple-element.23.guess, bf16[8,16,64,64]{3,2,1,0:T(8,128)(2,1)} %inv.3, f32[8,16,64,64]{3,2,1,0:T(8,128)} %border.3, bf16[4096,128]{1,0:T(8,128)(2,1)} %bitcast.22), custom_call_target="tpu_custom_call" | custom-call | tf_op jit(solution)/shard_map/step_windows/pallas_call | solution.py:134
  78.5 26.1 %image_exact.1 = (f32[8,16,64,128]{3,2,1,0:T(8,128)}, f32[1,128]{1,0:T(1,128)}, f32[512,128]{1,0:T(8,128)}) custom-call(f32[4,2,512,128]{3,2,1,0:T(8,128)} %bitcast.17, f32[512,128]{1,0:T(8,128)} %bitcast.19, f32[512,128]{1,0:T(8,128)} %get-tuple-element.27.refs_2_, f32[512,1]{1,0:T(8,128)} %copy.12.refs_3_, f32[8,16,64,128]{3,2,1,0:T(8,128)} %get-tuple-element.28.refs_4_, ...), custom_call_target="tpu_custom_call" | custom-call | tf_op jit(solution)/shard_map/image_exact/pallas_call | solution.py:508
  104.6 12.0 %guess_windows.3 = (f32[8,16,64,128]{3,2,1,0:T(8,128)}, f32[8,16,64,128]{3,2,1,0:T(8,128)}, bf16[4096,128]{1,0:T(8,128)(2,1)}) custom-call(s32[8,16]{1,0:T(8,128)} %blk.3, f32[8,16,64,128]{3,2,1,0:T(8,128)} %refs_1_.3, f32[8,16,64,128]{3,2,1,0:T(8,128)} %get-tuple-element.31.refs_2_, f32[1,128]{1,0:T(1,128)} %get-tuple-element.30.refs_3_, ...), custom_call_target="tpu_custom_call" | custom-call | tf_op jit(solution)/shard_map/guess_windows/pallas_call | solution.py:118
  116.6 46.4 %schur_solve.3 = (f32[512,128]{1,0:T(8,128)}, bf16[4,2,512,128]{3,2,1,0:T(8,128)(2,1)}) custom-call(bf16[4,2,512,128]{3,2,1,0:T(8,128)(2,1)} %bitcast.20, f32[512,128]{1,0:T(8,128)} %get-tuple-element.34.first.refs_1_, bf16[4,512,4096]{2,1,0:T(8,128)(2,1)} %bitcast.15), custom_call_target="tpu_custom_call" | custom-call | tf_op jit(solution)/shard_map/schur_solve/pallas_call | solution.py:316
  163.0 16.8 %step_windows.3 = (f32[8,16,64,128]{3,2,1,0:T(8,128)}, f32[8,16,64,128]{3,2,1,0:T(8,128)}, f32[4096,128]{1,0:T(8,128)}) custom-call(s32[8,16]{1,0:T(8,128)} %blk.3, f32[8,16,64,128]{3,2,1,0:T(8,128)} %get-tuple-element.32.guess, bf16[8,16,64,64]{3,2,1,0:T(8,128)(2,1)} %inv.3, f32[8,16,64,64]{3,2,1,0:T(8,128)} %border.3, bf16[4096,128]{1,0:T(8,128)(2,1)} %bitcast.23), custom_call_target="tpu_custom_call" | custom-call | tf_op jit(solution)/shard_map/step_windows/pallas_call | solution.py:134
  179.8 0.0 copy-start.3
  179.8 22.7 %image_sums.1 = (f32[1,128]{1,0:T(1,128)}, f32[512,128]{1,0:T(8,128)}) custom-call(f32[4,2,512,128]{3,2,1,0:T(8,128)} %bitcast.16, f32[512,128]{1,0:T(8,128)} %get-tuple-element.34.first.refs_1_, f32[512,128]{1,0:T(8,128)} %get-tuple-element.37.refs_2_, f32[512,1]{1,0:T(8,128)} %copy.12.refs_3_, f32[8,16,64,128]{3,2,1,0:T(8,128)} %get-tuple-element.38.refs_4_, ...), custom_call_target="tpu_custom_call" | custom-call | tf_op jit(solution)/shard_map/image_sums/pallas_call | solution.py:508
  202.6 0.0 copy-done.3
  202.6 0.0 copy-start
  202.6 0.0 copy-start.1
  202.6 0.0 copy-start.4
  202.6 0.0 copy-start.2
  202.6 7.0 %multiply_add_fusion = f32[8,16,64,128]{3,2,1,0:T(8,128)} fusion(f32[8,16,64,128]{3,2,1,0:T(8,128)} %get-tuple-element.38.refs_4_, f32[8,16,64,128]{3,2,1,0:T(8,128)} %get-tuple-element.28.refs_4_, f32[128]{0:T(128)} %bitcast.28, f32[128]{0:T(128)S(1)} %bitcast.25), kind=kLoop, calls=%fused_computation | loop fusion | flops 3145728 | bytes 12583936 | tf_op jit(solution)/shard_map/add | solution.py:582
  209.6 0.0 copy-done
  209.6 0.0 copy-done.1
  209.6 0.0 copy-done.4
  209.6 0.7 add_bitcast_fusion
  210.4 0.0 copy-done.2
  210.4 0.7 copy.15
Async XLA Ops:
  179.8 22.7 %copy-start.3 = (f32[1,128]{1,0:T(1,128)S(1)}, f32[1,128]{1,0:T(1,128)}, u32[]{:S(2)}) copy-start(f32[1,128]{1,0:T(1,128)} %get-tuple-element.30.refs_3_) | copy-start | bytes 1540
  202.6 7.0 %copy-start = (f32[512,128]{1,0:T(8,128)S(1)}, f32[512,128]{1,0:T(8,128)}, u32[]{:S(2)}) copy-start(f32[512,128]{1,0:T(8,128)} %get-tuple-element.27.refs_2_) | copy-start | bytes 786436
  202.6 7.0 %copy-start.1 = (f32[512,128]{1,0:T(8,128)S(1)}, f32[512,128]{1,0:T(8,128)}, u32[]{:S(2)}) copy-start(f32[512,128]{1,0:T(8,128)} %get-tuple-element.37.refs_2_) | copy-start | bytes 786436
  202.6 7.0 %copy-start.4 = (f32[1,128]{1,0:T(1,128)S(1)}, f32[1,128]{1,0:T(1,128)}, u32[]{:S(2)}) copy-start(f32[1,128]{1,0:T(1,128)} %get-tuple-element.41) | copy-start | bytes 1540
  202.6 7.8 %copy-start.2 = (f32[512,128]{1,0:T(8,128)S(1)}, f32[512,128]{1,0:T(8,128)}, u32[]{:S(2)}) copy-start(f32[512,128]{1,0:T(8,128)} %get-tuple-element.42) | copy-start | bytes 786436

commit v3 on v2

--- a/solution.py
+++ b/solution.py
@@ -30,11 +30,20 @@
     return hi, (x - hi.astype(F32)).astype(BF16)
 
 
+def twice(x):
+    return jnp.concatenate([x, x], axis=0)
+
+
+def halves(x):
+    hi, lo = split(x)
+    return jnp.concatenate([hi.astype(F32), lo.astype(F32)], axis=1).astype(BF16)
+
+
 def guess_kernel(update, size, *refs):
     if update:
-        blk, res, image, scale, inv, border, res_out, guess, part, acc = refs
+        blk, res, image, scale, inv, turned, res_out, guess, part, acc = refs
     else:
-        blk, res, inv, border, guess, part, acc = refs
+        blk, res, inv, border, guess, part, plain, turned, acc = refs
     s = pl.program_id(0)
     count = res.shape[1]
 
@@ -48,11 +57,14 @@
         if update:
             value = value - scale[...] * image[0, w]
             res_out[0, w] = value
+        else:
+            plain[0, w] = halves(border[0, w])
+            turned[0, w] = halves(border[0, w].T)
         guesses.append(dot(inv[0, w], value.astype(BF16)))
     terms = []
     for w in range(count):
         guess[0, w] = guesses[w]
-        terms.append(dot_t(border[0, w].astype(BF16), guesses[w].astype(BF16)))
+        terms.append(dot(turned[0, w], twice(guesses[w].astype(BF16))))
     for w in range(count):
         rows = pl.ds(pl.multiple_of(blk[s, w] * size, size), size)
         acc[rows, :] += terms[w]
@@ -62,7 +74,7 @@
         part[...] = acc[...].astype(BF16)
 
 
-def step_kernel(size, blk, guess, inv, border, group, step, coupled, part):
+def step_kernel(size, blk, guess, inv, plain, turned, group, step, coupled, part):
     s = pl.program_id(0)
     count = guess.shape[1]
 
@@ -70,24 +82,18 @@
     def _():
         part[...] = jnp.zeros_like(part)
 
-    places, lifted, borders, terms = [], [], [], []
+    places, lifted, terms = [], [], []
     for w in range(count):
         rows = pl.ds(pl.multiple_of(blk[s, w] * size, size), size)
         places.append(rows)
-        first = group[rows, :]
-        hi, lo = split(border[0, w])
-        borders.append((hi, lo))
-        value = dot(hi, first) + dot(lo, first)
+        value = dot(plain[0, w], twice(group[rows, :]))
         coupled[0, w] = value
         lifted.append(value.astype(BF16))
     for w in range(count):
         value = guess[0, w] - dot(inv[0, w], lifted[w])
         step[0, w] = value
         vh, vl = split(value)
-        hi, lo = borders[w]
-        left = jnp.concatenate([hi, lo, hi], axis=0)
-        right = jnp.concatenate([vh, vh, vl], axis=0)
-        terms.append(dot_t(left, right))
+        terms.append(dot(turned[0, w], twice(vh)) + dot(turned[0, w], twice(vl)))
     for w in range(count):
         part[places[w], :] += terms[w]
 
@@ -115,6 +121,10 @@
     full = jax.ShapeDtypeStruct(res.shape, F32)
     outs = ([full] if update else []) + [full, jax.ShapeDtypeStruct((rows, width), BF16)]
     out_specs = ([field] if update else []) + [field, fixed((rows, width))]
+    if not update:
+        pieces = border.shape[:3] + (2 * size,)
+        outs += [jax.ShapeDtypeStruct(pieces, BF16)] * 2
+        out_specs += [by_scenario(pieces)] * 2
     return pl.pallas_call(
         functools.partial(guess_kernel, update, size),
         grid=(res.shape[0],),
@@ -127,19 +137,21 @@
     )(*ops)
 
 
-def step_call(blk, guess, inv, border, group):
+def step_call(blk, guess, inv, plain, turned, group):
     rows, width = group.shape
     field = by_scenario(guess.shape)
     full = jax.ShapeDtypeStruct(guess.shape, F32)
     return pl.pallas_call(
         functools.partial(step_kernel, guess.shape[2]),
         grid=(guess.shape[0],),
-        in_specs=[SMEM, field, by_scenario(inv.shape), by_scenario(border.shape), fixed(group.shape)],
+        in_specs=[SMEM, field, by_scenario(inv.shape)]
+        + [by_scenario(plain.shape)] * 2
+        + [fixed(group.shape)],
         out_specs=[field, field, fixed((rows, width))],
         out_shape=[full, full, jax.ShapeDtypeStruct((rows, width), F32)],
         compiler_params=pltpu.CompilerParams(vmem_limit_bytes=LIMIT),
         name="step_windows",
-    )(blk, guess, inv, border, group)
+    )(blk, guess, inv, plain, turned, group)
 
 
 def greet(devices):
@@ -183,30 +195,41 @@
     def __init__(self, at, part, pair, mixed, arrived, sems):
         self.at, self.part, self.pair, self.mixed, self.arrived = at, part, pair, mixed, arrived
         near_send, near_recv, far_send, far_recv = sems
-        self.near = remote(part.at[:, 1 - at.core], pair, near_send.at[0], near_recv.at[0], at.sibling)
+        self.order = list(range(1, at.chips)) + [0]
+        self.near = {
+            k: remote(
+                part.at[at.ahead(k), 1 - at.core], pair.at[k], near_send.at[k], near_recv.at[k], at.sibling
+            )
+            for k in self.order
+        }
         self.far = [
             remote(mixed.at[k], arrived.at[k], far_send.at[k], far_recv.at[k], at.peer(k))
             for k in range(1, at.chips)
         ]
 
-    def mix(self, chip):
-        return self.part[chip, self.at.core].astype(F32) + self.pair[chip].astype(F32)
+    def start(self):
+        for k in self.order:
+            self.near[k].start()
+
+    def mix(self, k):
+        self.near[k].wait_recv()
+        return self.part[self.at.ahead(k), self.at.core].astype(F32) + self.pair[k].astype(F32)
 
     def pass_on(self):
-        self.near.wait_recv()
         for k, far in enumerate(self.far, 1):
-            self.mixed[k] = self.mix(self.at.ahead(k)).astype(self.mixed.dtype)
+            self.mixed[k] = self.mix(k).astype(self.mixed.dtype)
             far.start()
 
     def total(self):
-        value = self.mix(self.at.chip)
+        value = self.mix(0)
         for k, far in enumerate(self.far, 1):
             far.wait_recv()
             value = value + self.arrived[k].astype(F32)
         return value
 
     def finish(self):
-        self.near.wait_send()
+        for k in self.order:
+            self.near[k].wait_send()
         for far in self.far:
             far.wait_send()
 
@@ -226,7 +249,7 @@
     greet(at.greeted())
     one = Scatter(at, part, pair1, mixed1, arrived1, (a1, b1, c1, d1))
     two = Scatter(at, partial, pair2, mixed2, arrived2, (a2, b2, c2, d2))
-    one.near.start()
+    one.start()
     one.pass_on()
     rhs[me_f] = (first[...] + one.total()).T.astype(BF16)
 
@@ -274,10 +297,12 @@
         for way in range(2):
             _, has, _, g = hop(t, way)
             pl.when(has)(functools.partial(multiply, g, False))
-    for q in range(chips):
+    for k in two.order:
+        q = at.ahead(k)
         partial[q, 1 - core] = acc[2 * q + 1 - core].astype(BF16)
-    two.near.start()
-    for q in range(chips):
+        two.near[k].start()
+    for k in two.order:
+        q = at.ahead(k)
         partial[q, core] = acc[2 * q + core].astype(BF16)
     two.pass_on()
     rounded = two.total().T.astype(BF16)
@@ -334,9 +359,9 @@
             pltpu.VMEM((chips, width, own), BF16),
             pltpu.VMEM(part.shape, BF16),
             dma((n_f,)),
-            dma((1,)), dma((1,)), dma((chips,)), dma((chips,)),
+            dma((chips,)), dma((chips,)), dma((chips,)), dma((chips,)),
             dma((2, n_f)), dma((2, n_f)),
-            dma((1,)), dma((1,)), dma((chips,)), dma((chips,)),
+            dma((chips,)), dma((chips,)), dma((chips,)), dma((chips,)),
             dma((chips,)), dma((chips,)), dma((chips,)), dma((chips,)),
         ],
         compiler_params=pltpu.CompilerParams(
@@ -376,7 +401,7 @@
     others = [(lax.rem(me_s + k, n_s), me_f) for k in range(1, n_s)]
     greet(others + [at.along(k) for k in range(1, n_f)])
     one = Scatter(at, part, pair, mixed, arrived, (a1, b1, c1, d1))
-    one.near.start()
+    one.start()
     before = remote(step.at[:, 0], halo.at[1], halo_send.at[1], halo_recv.at[1], (me_s, lax.rem(me_f + n_f - 1, n_f)))
     after = remote(
         step.at[:, count - 1], halo.at[0], halo_send.at[0], halo_recv.at[0], (me_s, lax.rem(me_f + 1, n_f))
@@ -527,7 +552,7 @@
             pltpu.VMEM((n_s, 16, width), F32),
             pltpu.VMEM((n_f, 16, width), F32),
             dma((scens, 5)),
-            dma((1,)), dma((1,)), dma((chips,)), dma((chips,)),
+            dma((chips,)), dma((chips,)), dma((chips,)), dma((chips,)),
             dma((2,)), dma((2,)),
             dma((n_s,)), dma((n_s,)),
             dma((n_f,)), dma((n_f,)),
@@ -562,14 +587,14 @@
     image = scale = scen_sol = first_sol = None
     for round_index in range(ROUNDS):
         if round_index == 0:
-            guess, part = guess_call(border_block, scen_res, diag_inverse, border, group_rows)
+            guess, part, plain, turned = guess_call(border_block, scen_res, diag_inverse, border, group_rows)
         else:
             scen_res, guess, part = guess_call(
-                border_block, scen_res, diag_inverse, border, group_rows, image, scale
+                border_block, scen_res, diag_inverse, turned, group_rows, image, scale
             )
         owned, group = solve_call(n_s, n_f, part.reshape(n_s // 2, 2, own_rows, width), first_res, schur)
         step, coupled, part = step_call(
-            border_block, guess, diag_inverse, border, group.reshape(group_rows, width)
+            border_block, guess, diag_inverse, plain, turned, group.reshape(group_rows, width)
         )
         last = round_index == ROUNDS - 1
         found = image_call(

time: 212 us -> 212 us (level)
  no operation moved by 1% of the time
where the time goes in v3:
time: 212 us; the launch traced here: 211 us
  Pallas kernels  201 us (95%)
  other arithmetic  7.74 us (4%)
  local copies, waits for them, and re-layouts  2.26 us (1%)
    pallas_call x2, Pallas kernels, solve_call(): pl.pallas_call(functools.partial(solve_kernel, n_s, n_f), in_specs=[VMEM,...  95.1 us
    pallas_call x2, Pallas kernels, image_call(): pl.pallas_call(functools.partial(image_kernel, n_s, n_f, exact), in_specs...  47.2 us
    pallas_call x2, Pallas kernels, step_call(): pl.pallas_call(functools.partial(step_kernel, guess.shape[2]), grid=(gues...  34.8 us
    pallas_call x2, Pallas kernels, guess_call(): pl.pallas_call(functools.partial(guess_kernel, update, size), grid=(res.s...  23.4 us
    add x1, other arithmetic, per_device(): scen_sol = scale * step if scen_sol is None else scen_sol + scale * step  7 us

profile of v3, /device:TPU:0, one launch (start us, length us, event | category | flops | bytes accessed | tf_op | source)
XLA Modules:
  0.0 211.3 jit_solution(7645503906464182110)
XLA Ops:
  0.6 1.5 copy.12.refs_3_
  2.2 11.9 %guess_windows.2 = (f32[8,16,64,128]{3,2,1,0:T(8,128)}, bf16[4096,128]{1,0:T(8,128)(2,1)}, bf16[8,16,64,128]{3,2,1,0:T(8,128)(2,1)}, bf16[8,16,64,128]{3,2,1,0:T(8,128)(2,1)}) custom-call(s32[8,16]{1,0:T(8,128)} %blk.3, f32[8,16,64,128]{3,2,1,0:T(8,128)} %refs_1_.3, bf16[8,16,64,64]{3,2,1,0:T(8,128)(2,1)} %inv.3, f32[8,16,64,64]{3,2,1,0:T(8,128)} %refs_3_.1), custom_call_target="tpu_custom_call" | custom-call | tf_op jit(solution)/shard_map/guess_windows/pallas_call | solution.py:128
  14.0 49.5 %schur_solve.2 = (f32[512,128]{1,0:T(8,128)}, bf16[4,2,512,128]{3,2,1,0:T(8,128)(2,1)}) custom-call(bf16[4,2,512,128]{3,2,1,0:T(8,128)(2,1)} %bitcast.20, f32[512,128]{1,0:T(8,128)} %bitcast.18, bf16[4,512,4096]{2,1,0:T(8,128)(2,1)} %bitcast.14), custom_call_target="tpu_custom_call" | custom-call | tf_op jit(solution)/shard_map/schur_solve/pallas_call | solution.py:341
  63.5 17.5 %step_windows.2 = (f32[8,16,64,128]{3,2,1,0:T(8,128)}, f32[8,16,64,128]{3,2,1,0:T(8,128)}, f32[4096,128]{1,0:T(8,128)}) custom-call(s32[8,16]{1,0:T(8,128)} %blk.3, f32[8,16,64,128]{3,2,1,0:T(8,128)} %get-tuple-element.25.guess, bf16[8,16,64,64]{3,2,1,0:T(8,128)(2,1)} %inv.3, bf16[8,16,64,128]{3,2,1,0:T(8,128)(2,1)} %get-tuple-element.26.plain, ...), custom_call_target="tpu_custom_call" | custom-call | tf_op jit(solution)/shard_map/step_windows/pallas_call | solution.py:144
  81.0 25.5 %image_exact.1 = (f32[8,16,64,128]{3,2,1,0:T(8,128)}, f32[1,128]{1,0:T(1,128)}, f32[512,128]{1,0:T(8,128)}) custom-call(f32[4,2,512,128]{3,2,1,0:T(8,128)} %bitcast.17, f32[512,128]{1,0:T(8,128)} %bitcast.19, f32[512,128]{1,0:T(8,128)} %get-tuple-element.31.refs_2_, f32[512,1]{1,0:T(8,128)} %copy.12.refs_3_, f32[8,16,64,128]{3,2,1,0:T(8,128)} %get-tuple-element.32.refs_4_, ...), custom_call_target="tpu_custom_call" | custom-call | tf_op jit(solution)/shard_map/image_exact/pallas_call | solution.py:533
  106.4 11.6 %guess_windows.3 = (f32[8,16,64,128]{3,2,1,0:T(8,128)}, f32[8,16,64,128]{3,2,1,0:T(8,128)}, bf16[4096,128]{1,0:T(8,128)(2,1)}) custom-call(s32[8,16]{1,0:T(8,128)} %blk.3, f32[8,16,64,128]{3,2,1,0:T(8,128)} %refs_1_.3, f32[8,16,64,128]{3,2,1,0:T(8,128)} %get-tuple-element.35.refs_2_, f32[1,128]{1,0:T(1,128)} %get-tuple-element.34.refs_3_, ...), custom_call_target="tpu_custom_call" | custom-call | tf_op jit(solution)/shard_map/guess_windows/pallas_call | solution.py:128
  118.0 45.6 %schur_solve.3 = (f32[512,128]{1,0:T(8,128)}, bf16[4,2,512,128]{3,2,1,0:T(8,128)(2,1)}) custom-call(bf16[4,2,512,128]{3,2,1,0:T(8,128)(2,1)} %bitcast.21, f32[512,128]{1,0:T(8,128)} %get-tuple-element.38.first.refs_1_, bf16[4,512,4096]{2,1,0:T(8,128)(2,1)} %bitcast.15), custom_call_target="tpu_custom_call" | custom-call | tf_op jit(solution)/shard_map/schur_solve/pallas_call | solution.py:341
  163.6 17.3 %step_windows.3 = (f32[8,16,64,128]{3,2,1,0:T(8,128)}, f32[8,16,64,128]{3,2,1,0:T(8,128)}, f32[4096,128]{1,0:T(8,128)}) custom-call(s32[8,16]{1,0:T(8,128)} %blk.3, f32[8,16,64,128]{3,2,1,0:T(8,128)} %get-tuple-element.36.guess, bf16[8,16,64,64]{3,2,1,0:T(8,128)(2,1)} %inv.3, bf16[8,16,64,128]{3,2,1,0:T(8,128)(2,1)} %get-tuple-element.26.plain, ...), custom_call_target="tpu_custom_call" | custom-call | tf_op jit(solution)/shard_map/step_windows/pallas_call | solution.py:144
  181.0 0.0 copy-start.3
  181.0 21.8 %image_sums.1 = (f32[1,128]{1,0:T(1,128)}, f32[512,128]{1,0:T(8,128)}) custom-call(f32[4,2,512,128]{3,2,1,0:T(8,128)} %bitcast.16, f32[512,128]{1,0:T(8,128)} %get-tuple-element.38.first.refs_1_, f32[512,128]{1,0:T(8,128)} %get-tuple-element.41.refs_2_, f32[512,1]{1,0:T(8,128)} %copy.12.refs_3_, f32[8,16,64,128]{3,2,1,0:T(8,128)} %get-tuple-element.42.refs_4_, ...), custom_call_target="tpu_custom_call" | custom-call | tf_op jit(solution)/shard_map/image_sums/pallas_call | solution.py:533
  202.7 0.0 copy-done.3
  202.8 0.0 copy-start
  202.8 0.0 copy-start.1
  202.8 0.0 copy-start.4
  202.8 0.0 copy-start.2
  202.8 7.0 %multiply_add_fusion = f32[8,16,64,128]{3,2,1,0:T(8,128)} fusion(f32[8,16,64,128]{3,2,1,0:T(8,128)} %get-tuple-element.42.refs_4_, f32[8,16,64,128]{3,2,1,0:T(8,128)} %get-tuple-element.32.refs_4_, f32[128]{0:T(128)} %bitcast.28, f32[128]{0:T(128)S(1)} %bitcast.25), kind=kLoop, calls=%fused_computation | loop fusion | flops 3145728 | bytes 12583936 | tf_op jit(solution)/shard_map/add | solution.py:607
  209.8 0.0 copy-done
  209.8 0.0 copy-done.1
  209.8 0.0 copy-done.4
  209.8 0.7 add_bitcast_fusion
  210.5 0.0 copy-done.2
  210.6 0.7 copy.15
Async XLA Ops:
  181.0 21.8 %copy-start.3 = (f32[1,128]{1,0:T(1,128)S(1)}, f32[1,128]{1,0:T(1,128)}, u32[]{:S(2)}) copy-start(f32[1,128]{1,0:T(1,128)} %get-tuple-element.34.refs_3_) | copy-start | bytes 1540
  202.8 7.0 %copy-start = (f32[512,128]{1,0:T(8,128)S(1)}, f32[512,128]{1,0:T(8,128)}, u32[]{:S(2)}) copy-start(f32[512,128]{1,0:T(8,128)} %get-tuple-element.31.refs_2_) | copy-start | bytes 786436
  202.8 7.0 %copy-start.1 = (f32[512,128]{1,0:T(8,128)S(1)}, f32[512,128]{1,0:T(8,128)}, u32[]{:S(2)}) copy-start(f32[512,128]{1,0:T(8,128)} %get-tuple-element.41.refs_2_) | copy-start | bytes 786436
  202.8 7.0 %copy-start.4 = (f32[1,128]{1,0:T(1,128)S(1)}, f32[1,128]{1,0:T(1,128)}, u32[]{:S(2)}) copy-start(f32[1,128]{1,0:T(1,128)} %get-tuple-element.45) | copy-start | bytes 1540
  202.8 7.8 %copy-start.2 = (f32[512,128]{1,0:T(8,128)S(1)}, f32[512,128]{1,0:T(8,128)}, u32[]{:S(2)}) copy-start(f32[512,128]{1,0:T(8,128)} %get-tuple-element.46) | copy-start | bytes 786436

commit v4 on v3

--- a/solution.py
+++ b/solution.py
@@ -8,6 +8,7 @@
 from jax.sharding import PartitionSpec as P
 
 ROUNDS = 2
+PIECES = 2
 LIMIT = 60 * 1024 * 1024
 MESH = pl.DeviceIdType.MESH
 F32 = jnp.float32
@@ -56,7 +57,7 @@
         value = res[0, w]
         if update:
             value = value - scale[...] * image[0, w]
-            res_out[0, w] = value
+            res_out[0, w] = value.astype(BF16)
         else:
             plain[0, w] = halves(border[0, w])
             turned[0, w] = halves(border[0, w].T)
@@ -119,7 +120,7 @@
     specs = [SMEM, field] + ([field, fixed(scale.shape)] if update else [])
     specs += [by_scenario(inv.shape), by_scenario(border.shape)]
     full = jax.ShapeDtypeStruct(res.shape, F32)
-    outs = ([full] if update else []) + [full, jax.ShapeDtypeStruct((rows, width), BF16)]
+    outs = ([jax.ShapeDtypeStruct(res.shape, BF16)] if update else []) + [full, jax.ShapeDtypeStruct((rows, width), BF16)]
     out_specs = ([field] if update else []) + [field, fixed((rows, width))]
     if not update:
         pieces = border.shape[:3] + (2 * size,)
@@ -247,31 +248,39 @@
     for load in loads:
         load.start()
     greet(at.greeted())
-    one = Scatter(at, part, pair1, mixed1, arrived1, (a1, b1, c1, d1))
+    half = own // PIECES
+    bands = [pl.ds(h * half, half) for h in range(PIECES)]
+    ones = [
+        Scatter(
+            at, part.at[:, :, bands[h]], pair1.at[h], mixed1.at[h], arrived1.at[h],
+            (a1.at[h], b1.at[h], c1.at[h], d1.at[h]),
+        )
+        for h in range(PIECES)
+    ]
     two = Scatter(at, partial, pair2, mixed2, arrived2, (a2, b2, c2, d2))
-    one.start()
-    one.pass_on()
-    rhs[me_f] = (first[...] + one.total()).T.astype(BF16)
+    for one in ones:
+        one.start()
+    for one in ones:
+        one.pass_on()
 
     def hop(t, way):
         g = lax.rem(me_f + (t if way else n_f - t), n_f)
-        copy = functools.partial(
-            remote, rhs.at[g], rhs.at[g], line_send.at[way, t], line_recv.at[way, t + 1], at.along(n_f - 1 if way else 1)
-        )
         has = (me_f + t < n_f) if way else (me_f - t >= 0)
         more = (me_f > 0) if way else (me_f < n_f - 1)
-        return copy, has, jnp.logical_and(has, more), g
-
-    def send(t):
+        return g, has, jnp.logical_and(has, more)
+
+    def moved(h, t, way, later):
+        spot = rhs.at[hop(t, way)[0], h]
+        to = at.along(n_f - 1 if way else 1)
+        return remote(spot, spot, line_send.at[h, way, t], line_recv.at[h, way, t + later], to)
+
+    def send(h, t):
         for way in range(2):
-            copy, has, goes, g = hop(t, way)
+            _, has, goes = hop(t, way)
             if t > 0:
-                arrival = remote(
-                    rhs.at[g], rhs.at[g], line_send.at[way, t], line_recv.at[way, t], at.along(1)
-                )
-                pl.when(has)(arrival.wait_recv)
+                pl.when(has)(lambda way=way: moved(h, t, way, 0).wait_recv())
             if t < n_f - 1:
-                pl.when(goes)(lambda copy=copy: copy().start())
+                pl.when(goes)(lambda way=way: moved(h, t, way, 1).start())
 
     def multiply(g, begin):
         if aligned:
@@ -279,24 +288,36 @@
             @pl.loop(0, n_s)
             def _(p):
                 columns = pl.ds(pl.multiple_of(p * own, 128), own)
-                value = dot(rhs[g], mats[g, :, columns])
+                value = dot(rhs[g, 0], mats[g, bands[0], columns])
+                for h in range(1, PIECES):
+                    value = value + dot(rhs[g, h], mats[g, bands[h], columns])
                 acc[p] = value if begin else acc[p] + value
 
         else:
-            value = dot(rhs[g], mats[g])
+            value = dot(rhs[g, 0], mats[g, bands[0]])
+            for h in range(1, PIECES):
+                value = value + dot(rhs[g, h], mats[g, bands[h]])
             for p in range(n_s):
                 piece = value[:, p * own : (p + 1) * own]
                 acc[p] = piece if begin else acc[p] + piece
 
-    send(0)
+    for h, one in enumerate(ones):
+        rhs[me_f, h] = (first[bands[h]] + one.total()).T.astype(BF16)
+        send(h, 0)
     for load in loads:
         load.wait()
     multiply(me_f, True)
     for t in range(1, n_f):
-        send(t)
-        for way in range(2):
-            _, has, _, g = hop(t, way)
-            pl.when(has)(functools.partial(multiply, g, False))
+        for h in range(PIECES):
+            send(h, t)
+        left, from_left, _ = hop(t, 0)
+        right, from_right, _ = hop(t, 1)
+        pl.when(from_left)(functools.partial(multiply, left, False))
+        alone = jnp.logical_and(from_right, me_f < t)
+        pl.when(alone)(functools.partial(multiply, right, False))
+    for t in range(1, n_f // 2 + n_f % 2):
+        both = jnp.logical_and(hop(t, 0)[1], hop(t, 1)[1])
+        pl.when(both)(functools.partial(multiply, hop(t, 1)[0], False))
     for k in two.order:
         q = at.ahead(k)
         partial[q, 1 - core] = acc[2 * q + 1 - core].astype(BF16)
@@ -324,19 +345,21 @@
         spot = steps.at[at.behind(k), 1 - core]
         remote(spot, spot, near_send.at[k], near_recv.at[k], at.sibling).wait_recv()
     group[...] = steps[...]
-    one.finish()
+    for one in ones:
+        one.finish()
     two.finish()
     for copy in across + over:
         copy.wait_send()
     for t in range(n_f - 1):
         for way in range(2):
-            copy, _, goes, _ = hop(t, way)
-            pl.when(goes)(lambda copy=copy: copy().wait_send())
+            for h in range(PIECES):
+                pl.when(hop(t, way)[2])(lambda h=h, t=t, way=way: moved(h, t, way, 1).wait_send())
 
 
 def solve_call(n_s, n_f, part, first, schur):
     own, width = first.shape
     chips = n_s // 2
+    banded = (PIECES, chips, own // PIECES, width)
     dma = pltpu.SemaphoreType.DMA
     return pl.pallas_call(
         functools.partial(solve_kernel, n_s, n_f),
@@ -348,10 +371,10 @@
         ],
         scratch_shapes=[
             pltpu.VMEM(schur.shape, BF16),
-            pltpu.VMEM((chips, own, width), BF16),
-            pltpu.VMEM((chips, own, width), BF16),
-            pltpu.VMEM((chips, own, width), BF16),
-            pltpu.VMEM((n_f, width, own), BF16),
+            pltpu.VMEM(banded, BF16),
+            pltpu.VMEM(banded, BF16),
+            pltpu.VMEM(banded, BF16),
+            pltpu.VMEM((n_f, PIECES, width, own // PIECES), BF16),
             pltpu.VMEM((n_s, width, own), F32),
             pltpu.VMEM((chips, 2, width, own), BF16),
             pltpu.VMEM((chips, width, own), BF16),
@@ -359,8 +382,8 @@
             pltpu.VMEM((chips, width, own), BF16),
             pltpu.VMEM(part.shape, BF16),
             dma((n_f,)),
-            dma((chips,)), dma((chips,)), dma((chips,)), dma((chips,)),
-            dma((2, n_f)), dma((2, n_f)),
+            dma((PIECES, chips)), dma((PIECES, chips)), dma((PIECES, chips)), dma((PIECES, chips)),
+            dma((PIECES, 2, n_f)), dma((PIECES, 2, n_f)),
             dma((chips,)), dma((chips,)), dma((chips,)), dma((chips,)),
             dma((chips,)), dma((chips,)), dma((chips,)), dma((chips,)),
         ],
@@ -434,7 +457,7 @@
             value = value + v_coupled[s, w]
             if exact:
                 image[s, w] = value
-            a = a + fold(v_res[s, w] * value)
+            a = a + fold(v_res[s, w].astype(F32) * value)
             e = e + fold(value * value)
         along[...] = a
         energy[...] = e
@@ -541,7 +564,7 @@
             pltpu.VMEM((chips, own, width), FAR),
             pltpu.VMEM((2, scens, size, width), F32),
             pltpu.VMEM(step.shape, F32),
-            pltpu.VMEM(res.shape, F32),
+            pltpu.VMEM(res.shape, res.dtype),
             pltpu.VMEM(coupled.shape, F32),
             pltpu.VMEM(diag.shape, F32),
             pltpu.VMEM(pairs.shape, F32),

time: 212 us -> 206 us (0.972)
  Pallas kernels: 201 us -> 194 us
    pallas_call x2, Pallas kernels: 95.1 us -> 89.4 us  [solve_call(): pl.pallas_call(functools.partial(solve_kernel, n_s, n_f), in_specs=[VMEM,...]
where the time goes in v4:
time: 206 us; the launch traced here: 205 us
  Pallas kernels  194 us (94%)
  other arithmetic  7.74 us (4%)
  local copies, waits for them, and re-layouts  2.26 us (1%)
    pallas_call x2, Pallas kernels, solve_call(): pl.pallas_call(functools.partial(solve_kernel, n_s, n_f), in_specs=[VMEM,...  89.4 us
    pallas_call x2, Pallas kernels, image_call(): pl.pallas_call(functools.partial(image_kernel, n_s, n_f, exact), in_specs...  47.2 us
    pallas_call x2, Pallas kernels, step_call(): pl.pallas_call(functools.partial(step_kernel, guess.shape[2]), grid=(gues...  34.7 us
    pallas_call x2, Pallas kernels, guess_call(): pl.pallas_call(functools.partial(guess_kernel, update, size), grid=(res.s...  22.9 us
    add x1, other arithmetic, per_device(): scen_sol = scale * step if scen_sol is None else scen_sol + scale * step  7 us

profile of v4, /device:TPU:0, one launch (start us, length us, event | category | flops | bytes accessed | tf_op | source)
XLA Modules:
  0.0 204.9 jit_solution(5491093969256677335)
XLA Ops:
  0.6 1.5 copy.12.refs_3_
  2.2 11.9 %guess_windows.2 = (f32[8,16,64,128]{3,2,1,0:T(8,128)}, bf16[4096,128]{1,0:T(8,128)(2,1)}, bf16[8,16,64,128]{3,2,1,0:T(8,128)(2,1)}, bf16[8,16,64,128]{3,2,1,0:T(8,128)(2,1)}) custom-call(s32[8,16]{1,0:T(8,128)} %blk.3, f32[8,16,64,128]{3,2,1,0:T(8,128)} %refs_1_.3, bf16[8,16,64,64]{3,2,1,0:T(8,128)(2,1)} %inv.3, f32[8,16,64,64]{3,2,1,0:T(8,128)} %refs_3_.1), custom_call_target="tpu_custom_call" | custom-call | tf_op jit(solution)/shard_map/guess_windows/pallas_call | solution.py:129
  14.1 46.9 %schur_solve.2 = (f32[512,128]{1,0:T(8,128)}, bf16[4,2,512,128]{3,2,1,0:T(8,128)(2,1)}) custom-call(bf16[4,2,512,128]{3,2,1,0:T(8,128)(2,1)} %bitcast.20, f32[512,128]{1,0:T(8,128)} %bitcast.18, bf16[4,512,4096]{2,1,0:T(8,128)(2,1)} %bitcast.14), custom_call_target="tpu_custom_call" | custom-call | tf_op jit(solution)/shard_map/schur_solve/pallas_call | solution.py:364
  61.0 17.4 %step_windows.2 = (f32[8,16,64,128]{3,2,1,0:T(8,128)}, f32[8,16,64,128]{3,2,1,0:T(8,128)}, f32[4096,128]{1,0:T(8,128)}) custom-call(s32[8,16]{1,0:T(8,128)} %blk.3, f32[8,16,64,128]{3,2,1,0:T(8,128)} %get-tuple-element.25.guess, bf16[8,16,64,64]{3,2,1,0:T(8,128)(2,1)} %inv.3, bf16[8,16,64,128]{3,2,1,0:T(8,128)(2,1)} %get-tuple-element.26.plain, ...), custom_call_target="tpu_custom_call" | custom-call | tf_op jit(solution)/shard_map/step_windows/pallas_call | solution.py:145
  78.3 25.5 %image_exact.1 = (f32[8,16,64,128]{3,2,1,0:T(8,128)}, f32[1,128]{1,0:T(1,128)}, f32[512,128]{1,0:T(8,128)}) custom-call(f32[4,2,512,128]{3,2,1,0:T(8,128)} %bitcast.17, f32[512,128]{1,0:T(8,128)} %bitcast.19, f32[512,128]{1,0:T(8,128)} %get-tuple-element.31.refs_2_, f32[512,1]{1,0:T(8,128)} %copy.12.refs_3_, f32[8,16,64,128]{3,2,1,0:T(8,128)} %get-tuple-element.32.refs_4_, ...), custom_call_target="tpu_custom_call" | custom-call | tf_op jit(solution)/shard_map/image_exact/pallas_call | solution.py:556
  103.9 11.0 %guess_windows.3 = (bf16[8,16,64,128]{3,2,1,0:T(8,128)(2,1)}, f32[8,16,64,128]{3,2,1,0:T(8,128)}, bf16[4096,128]{1,0:T(8,128)(2,1)}) custom-call(s32[8,16]{1,0:T(8,128)} %blk.3, f32[8,16,64,128]{3,2,1,0:T(8,128)} %refs_1_.3, f32[8,16,64,128]{3,2,1,0:T(8,128)} %get-tuple-element.35.refs_2_, f32[1,128]{1,0:T(1,128)} %get-tuple-element.34.refs_3_, ...), custom_call_target="tpu_custom_call" | custom-call | tf_op jit(solution)/shard_map/guess_windows/pallas_call | solution.py:129
  114.8 42.4 %schur_solve.3 = (f32[512,128]{1,0:T(8,128)}, bf16[4,2,512,128]{3,2,1,0:T(8,128)(2,1)}) custom-call(bf16[4,2,512,128]{3,2,1,0:T(8,128)(2,1)} %bitcast.21, f32[512,128]{1,0:T(8,128)} %get-tuple-element.38.first.refs_1_, bf16[4,512,4096]{2,1,0:T(8,128)(2,1)} %bitcast.15), custom_call_target="tpu_custom_call" | custom-call | tf_op jit(solution)/shard_map/schur_solve/pallas_call | solution.py:364
  157.3 17.4 %step_windows.3 = (f32[8,16,64,128]{3,2,1,0:T(8,128)}, f32[8,16,64,128]{3,2,1,0:T(8,128)}, f32[4096,128]{1,0:T(8,128)}) custom-call(s32[8,16]{1,0:T(8,128)} %blk.3, f32[8,16,64,128]{3,2,1,0:T(8,128)} %get-tuple-element.36.guess, bf16[8,16,64,64]{3,2,1,0:T(8,128)(2,1)} %inv.3, bf16[8,16,64,128]{3,2,1,0:T(8,128)(2,1)} %get-tuple-element.26.plain, ...), custom_call_target="tpu_custom_call" | custom-call | tf_op jit(solution)/shard_map/step_windows/pallas_call | solution.py:145
  174.7 0.0 copy-start.3
  174.7 21.7 %image_sums.1 = (f32[1,128]{1,0:T(1,128)}, f32[512,128]{1,0:T(8,128)}) custom-call(f32[4,2,512,128]{3,2,1,0:T(8,128)} %bitcast.16, f32[512,128]{1,0:T(8,128)} %get-tuple-element.38.first.refs_1_, f32[512,128]{1,0:T(8,128)} %get-tuple-element.41.refs_2_, f32[512,1]{1,0:T(8,128)} %copy.12.refs_3_, f32[8,16,64,128]{3,2,1,0:T(8,128)} %get-tuple-element.42.refs_4_, ...), custom_call_target="tpu_custom_call" | custom-call | tf_op jit(solution)/shard_map/image_sums/pallas_call | solution.py:556
  196.4 0.0 copy-done.3
  196.4 0.0 copy-start
  196.4 0.0 copy-start.1
  196.4 0.0 copy-start.4
  196.4 0.0 copy-start.2
  196.5 7.0 %multiply_add_fusion = f32[8,16,64,128]{3,2,1,0:T(8,128)} fusion(f32[8,16,64,128]{3,2,1,0:T(8,128)} %get-tuple-element.42.refs_4_, f32[8,16,64,128]{3,2,1,0:T(8,128)} %get-tuple-element.32.refs_4_, f32[128]{0:T(128)} %bitcast.28, f32[128]{0:T(128)S(1)} %bitcast.25), kind=kLoop, calls=%fused_computation | loop fusion | flops 3145728 | bytes 12583936 | tf_op jit(solution)/shard_map/add | solution.py:630
  203.5 0.0 copy-done
  203.5 0.0 copy-done.1
  203.5 0.0 copy-done.4
  203.5 0.7 add_bitcast_fusion
  204.2 0.0 copy-done.2
  204.2 0.7 copy.15
Async XLA Ops:
  174.7 21.7 %copy-start.3 = (f32[1,128]{1,0:T(1,128)S(1)}, f32[1,128]{1,0:T(1,128)}, u32[]{:S(2)}) copy-start(f32[1,128]{1,0:T(1,128)} %get-tuple-element.34.refs_3_) | copy-start | bytes 1540
  196.4 7.0 %copy-start = (f32[512,128]{1,0:T(8,128)S(1)}, f32[512,128]{1,0:T(8,128)}, u32[]{:S(2)}) copy-start(f32[512,128]{1,0:T(8,128)} %get-tuple-element.31.refs_2_) | copy-start | bytes 786436
  196.4 7.0 %copy-start.1 = (f32[512,128]{1,0:T(8,128)S(1)}, f32[512,128]{1,0:T(8,128)}, u32[]{:S(2)}) copy-start(f32[512,128]{1,0:T(8,128)} %get-tuple-element.41.refs_2_) | copy-start | bytes 786436
  196.4 7.0 %copy-start.4 = (f32[1,128]{1,0:T(1,128)S(1)}, f32[1,128]{1,0:T(1,128)}, u32[]{:S(2)}) copy-start(f32[1,128]{1,0:T(1,128)} %get-tuple-element.45) | copy-start | bytes 1540
  196.4 7.8 %copy-start.2 = (f32[512,128]{1,0:T(8,128)S(1)}, f32[512,128]{1,0:T(8,128)}, u32[]{:S(2)}) copy-start(f32[512,128]{1,0:T(8,128)} %get-tuple-element.46) | copy-start | bytes 786436
